TPU v7x, 256 devices: a whole 4x4x8 slice. The times are simulated.
256 devices in a mesh: gx: 32 (over y_hi, z, core), gy: 8 (over y_lo, x).
Axes of the slice: x: 4, y: 4 (y_hi: 2, y_lo: 2; y = y_hi * 2 + y_lo), z: 8, core: 2. Of those that a mesh axis runs over, the one named last changes fastest.
Arguments:
- positions: float32 [3, 524288], P(None, ('gx', 'gy')), may hold values from 0 to 6
- features: bfloat16 [64, 524288], P(None, ('gx', 'gy')), may hold values from -6 to 6
- halo_lists: int32 [2, 393216], P(None, ('gx', 'gy')), may hold values from 0 to 2047
- local_pairs: int32 [4, 1572864], P(None, ('gx', 'gy')), may hold values from 0 to 2047, as said below
- cross_x: int32 [4, 524288], P(None, ('gx', 'gy')), may hold values from 0 to 2047, as said below
- cross_y: int32 [4, 524288], P(None, ('gx', 'gy')), may hold values from 0 to 2047, as said below
- pair_counts: int32 [256, 3], P(('gx', 'gy')), may hold values from 256 to 6144, as said below
- w_rbf: bfloat16 [8, 256], replicated, may hold values from -2 to 2
- w_src: bfloat16 [64, 256], replicated, may hold values from -0.75 to 0.75
- w_dst: bfloat16 [64, 256], replicated, may hold values from -0.75 to 0.75
- species_src: bfloat16 [4, 256], replicated, may hold values from -3 to 3
- species_dst: bfloat16 [4, 256], replicated, may hold values from -3 to 3
- w_hidden: bfloat16 [256, 256], replicated, may hold values from -0.375 to 0.375
- w_latent: bfloat16 [256, 64], replicated, may hold values from -0.375 to 0.375
- w_energy: float32 [64], replicated, may hold values from -0.75 to 0.75
Outputs:
- energy: float32 [1], replicated
- forces: float32 [3, 524288], P(None, ('gx', 'gy'))
- feature_grads: float32 [64, 524288], P(None, ('gx', 'gy'))
Inputs may be any that keep to these rules, and one draw needn't show every extreme that they name: `local_pairs`: rows 0 and 1 are different atoms of the block, below 2048; rows 2 and 3 are species below 4. `cross_x`: row 0 an atom below 2048, row 1 a slot below 1536, rows 2 and 3 species below 4. `cross_y`: row 0 an atom below 2048, row 1 a slot below 1536, rows 2 and 3 species below 4. `pair_counts`: column 0 counts live slots of local_pairs (at most 6144), columns 1 and 2 those of cross_x and cross_y (at most 2048); live slots come first; some device is full in each column.
All inputs are finite; a program needn't handle non-finite values.
Results may differ from a plain program's by a relative error of at most 0.0095.
Values may be sent and summed in bfloat16 or wider, within the bound.
A program may use at most 64 MiB of HBM per device.

v0:
```python
import jax
import jax.numpy as jnp
from jax import lax
from jax.sharding import PartitionSpec as P

BLOCK = 512


cutoff_radius = 6.0
block_edge = 6.0
softening = 0.1


def shifted(array, axis, by):
    length = lax.axis_size(axis)
    return lax.ppermute(array, axis, [(i, (i + by) % length) for i in range(length)])


def pair_energy(
    src_pos, src_feat, dst_pos, dst_feat, spec_src, spec_dst, live_mask, offset, weights
):
    w_rbf, w_src, w_dst, species_src, species_dst, w_hidden, w_latent, w_energy = weights
    displace = dst_pos + offset[:, None] - src_pos
    radius = jnp.sqrt(jnp.sum(displace * displace, axis=0) + softening)
    orders = jnp.arange(1, w_rbf.shape[0] + 1).astype(jnp.float32)[:, None]
    basis = (jnp.sin(orders * (jnp.pi / cutoff_radius) * radius[None, :]) / radius[None, :]).astype(
        jnp.bfloat16
    )
    kinds = jnp.arange(species_src.shape[0], dtype=jnp.int32)[:, None]
    onehot_src = (spec_src[None, :] == kinds).astype(jnp.bfloat16)
    onehot_dst = (spec_dst[None, :] == kinds).astype(jnp.bfloat16)
    pre = jnp.dot(w_rbf.T, basis, preferred_element_type=jnp.float32)
    pre = pre + jnp.dot(w_src.T, src_feat.astype(jnp.bfloat16), preferred_element_type=jnp.float32)
    pre = pre + jnp.dot(w_dst.T, dst_feat.astype(jnp.bfloat16), preferred_element_type=jnp.float32)
    pre = pre + jnp.dot(species_src.T, onehot_src, preferred_element_type=jnp.float32)
    pre = pre + jnp.dot(species_dst.T, onehot_dst, preferred_element_type=jnp.float32)
    hidden = jax.nn.silu(pre).astype(jnp.bfloat16)
    second = jax.nn.silu(jnp.dot(w_hidden.T, hidden, preferred_element_type=jnp.float32)).astype(
        jnp.bfloat16
    )
    latent = jnp.dot(w_latent.T, second, preferred_element_type=jnp.float32)
    ratio = jnp.minimum(radius / cutoff_radius, 1.0)
    envelope = (1.0 - ratio**2) ** 2
    scores = jnp.dot(w_energy, latent, precision=lax.Precision.HIGHEST)
    return jnp.sum(envelope * scores * live_mask)


def block_grads(
    src_pos, src_feat, dst_pos, dst_feat, spec_src, spec_dst, live_mask, offset, weights
):

    def energy_of(pos_one, feat_one, pos_two, feat_two):
        return pair_energy(
            pos_one, feat_one, pos_two, feat_two, spec_src, spec_dst, live_mask, offset, weights
        )

    energy, pullback = jax.vjp(
        energy_of, src_pos, src_feat.astype(jnp.float32), dst_pos, dst_feat.astype(jnp.float32)
    )
    return (energy, pullback(jnp.ones_like(energy)))


def to_blocks(array):
    count = array.shape[-1] // BLOCK
    if array.ndim == 1:
        return array.reshape(count, BLOCK)
    return jnp.moveaxis(array.reshape(array.shape[0], count, BLOCK), 1, 0)


def from_blocks(array):
    return jnp.moveaxis(array, 0, 1).reshape(array.shape[1], -1)


def run_edges(src_pos, src_feat, dst_pos, dst_feat, spec_src, spec_dst, live_mask, offset, weights):
    inputs = (src_pos, src_feat, dst_pos, dst_feat, spec_src, spec_dst, live_mask)

    def visit(total, blocks):
        energy, grads = block_grads(*blocks, offset, weights)
        return (total + energy, grads)

    total, grads = lax.scan(
        visit, jnp.zeros((), jnp.float32), tuple((to_blocks(item) for item in inputs))
    )
    return (total, tuple((from_blocks(item) for item in grads)))


def on_device(
    positions,
    features,
    halo_lists,
    local_pairs,
    cross_x,
    cross_y,
    pair_counts,
    w_rbf,
    w_src,
    w_dst,
    species_src,
    species_dst,
    w_hidden,
    w_latent,
    w_energy,
):
    weights = (w_rbf, w_src, w_dst, species_src, species_dst, w_hidden, w_latent, w_energy)
    atoms = positions.shape[1]
    halo_size = halo_lists.shape[1]
    width = features.shape[0]
    list_x = halo_lists[0]
    list_y = halo_lists[1]
    got_pos_x = shifted(positions[:, list_x], "gx", -1)
    got_feat_x = shifted(features[:, list_x], "gx", -1)
    got_pos_y = shifted(positions[:, list_y], "gy", -1)
    got_feat_y = shifted(features[:, list_y], "gy", -1)
    zero_off = jnp.zeros((3,), jnp.float32)
    off_x = jnp.array([block_edge, 0.0, 0.0], jnp.float32)
    off_y = jnp.array([0.0, block_edge, 0.0], jnp.float32)
    counts = pair_counts[0]
    slots_loc = jnp.arange(local_pairs.shape[1], dtype=jnp.int32)
    slots_cross = jnp.arange(cross_x.shape[1], dtype=jnp.int32)
    live_loc = (slots_loc < counts[0]).astype(jnp.float32)
    flag_x = (slots_cross < counts[1]).astype(jnp.int32)
    flag_y = (slots_cross < counts[2]).astype(jnp.int32)
    source, target = (local_pairs[0], local_pairs[1])
    energy_loc, grads = run_edges(
        positions[:, source],
        features[:, source],
        positions[:, target],
        features[:, target],
        local_pairs[2],
        local_pairs[3],
        live_loc,
        zero_off,
        weights,
    )
    grad_pos = (
        jnp.zeros((3, atoms), jnp.float32).at[:, source].add(grads[0]).at[:, target].add(grads[2])
    )
    grad_feat = (
        jnp.zeros((width, atoms), jnp.float32)
        .at[:, source]
        .add(grads[1])
        .at[:, target]
        .add(grads[3])
    )
    source_x, slot_x = (cross_x[0], cross_x[1])
    src_pos_x = positions[:, source_x]
    src_feat_x = features[:, source_x]
    energy_x, grads_x = run_edges(
        src_pos_x,
        src_feat_x,
        got_pos_x[:, slot_x],
        got_feat_x[:, slot_x],
        cross_x[2],
        cross_x[3],
        flag_x.astype(jnp.float32),
        off_x,
        weights,
    )
    grad_pos = grad_pos.at[:, source_x].add(grads_x[0])
    grad_feat = grad_feat.at[:, source_x].add(grads_x[1])
    source_y, slot_y = (cross_y[0], cross_y[1])
    src_pos_y = positions[:, source_y]
    src_feat_y = features[:, source_y]
    energy_y, grads_y = run_edges(
        src_pos_y,
        src_feat_y,
        got_pos_y[:, slot_y],
        got_feat_y[:, slot_y],
        cross_y[2],
        cross_y[3],
        flag_y.astype(jnp.float32),
        off_y,
        weights,
    )
    grad_pos = grad_pos.at[:, source_y].add(grads_y[0])
    grad_feat = grad_feat.at[:, source_y].add(grads_y[1])
    lent_pos_x = jnp.zeros((3, halo_size), jnp.float32).at[:, slot_x].add(grads_x[2])
    lent_feat_x = jnp.zeros((width, halo_size), jnp.float32).at[:, slot_x].add(grads_x[3])
    back_pos_x, back_feat_x = shifted((lent_pos_x, lent_feat_x), "gx", 1)
    lent_pos_y = jnp.zeros((3, halo_size), jnp.float32).at[:, slot_y].add(grads_y[2])
    lent_feat_y = jnp.zeros((width, halo_size), jnp.float32).at[:, slot_y].add(grads_y[3])
    back_pos_y, back_feat_y = shifted((lent_pos_y, lent_feat_y), "gy", 1)
    grad_pos = grad_pos.at[:, list_x].add(back_pos_x).at[:, list_y].add(back_pos_y)
    grad_feat = grad_feat.at[:, list_x].add(back_feat_x).at[:, list_y].add(back_feat_y)
    total = lax.psum(energy_loc + energy_x + energy_y, ("gx", "gy"))
    atoms_all = atoms * lax.axis_size("gx") * lax.axis_size("gy")
    energy = (total / atoms_all).reshape(1)
    return (energy, -grad_pos, grad_feat)


def solution(mesh):
    return jax.shard_map(
        on_device,
        mesh=mesh,
        in_specs=(
            P(None, ("gx", "gy")),
            P(None, ("gx", "gy")),
            P(None, ("gx", "gy")),
            P(None, ("gx", "gy")),
            P(None, ("gx", "gy")),
            P(None, ("gx", "gy")),
            P(("gx", "gy"), None),
            P(),
            P(),
            P(),
            P(),
            P(),
            P(),
            P(),
            P(),
        ),
        out_specs=(P(), P(None, ("gx", "gy")), P(None, ("gx", "gy"))),
        check_vma=False,
    )
```

profile of v0, /device:TPU:1, one launch (start us, length us, event | category | flops | bytes accessed | tf_op | source)
XLA Modules:
  0.0 808.5 jit_solution(13375963660446118232)
XLA Ops:
  2.7 2.6 gather_fusion.4
  5.5 3.3 collective-permute-start
  9.1 4.0 gather_fusion.8
  13.2 6.3 collective-permute-start.1
  19.4 2.6 gather_fusion.10
  22.9 2.6 collective-permute-start.2
  25.5 4.0 gather_fusion.14
  34.0 21.4 %gather_fusion.1 = f32[6144,3]{1,0:T(8,128)} fusion(f32[3,2048]{0,1:T(8,128)S(1)} %copy.90, s32[6144]{0:T(1024)S(1)} %broadcast_clamp_fusion), kind=kCustom, calls=%fused_computation.1 | custom fusion | bytes 172032 | tf_op jit(solution)/shard_map/gather | solution.py:125
  55.4 22.0 %gather_fusion.2 = bf16[6144,64]{1,0:T(8,128)(2,1)} fusion(bf16[64,2048]{0,1:T(8,128)(2,1)S(1)} %copy.94, s32[6144]{0:T(1024)S(1)} %broadcast_clamp_fusion), kind=kCustom, calls=%fused_computation.2 | custom fusion | bytes 1597440 | tf_op jit(solution)/shard_map/gather | solution.py:126
  77.5 20.9 %gather_fusion = f32[6144,3]{1,0:T(8,128)} fusion(f32[3,2048]{0,1:T(8,128)S(1)} %copy.90, s32[6144]{0:T(1024)S(1)} %broadcast_clamp_fusion.1), kind=kCustom, calls=%fused_computation | custom fusion | bytes 172032 | tf_op jit(solution)/shard_map/gather | solution.py:127
  98.3 22.1 %gather_fusion.3 = bf16[6144,64]{1,0:T(8,128)(2,1)} fusion(bf16[64,2048]{0,1:T(8,128)(2,1)S(1)} %copy.94, s32[6144]{0:T(1024)S(1)} %broadcast_clamp_fusion.1), kind=kCustom, calls=%fused_computation.3 | custom fusion | bytes 1597440 | tf_op jit(solution)/shard_map/gather | solution.py:128
  120.4 7.6 gather_fusion.6
  128.0 6.2 gather_fusion.7
  134.2 7.6 gather_fusion.12
  141.7 8.0 gather_fusion.13
  149.8 3.0 copy.91
  152.7 3.1 copy.93
  157.2 2.5 copy.97
  164.4 7.6 gather_fusion.5
  174.5 7.6 gather_fusion.11
  183.7 6.2 gather_fusion.9
  190.3 35.0 %while.57 = (s32[]{:T(128)}, f32[]{:T(128)}, f32[4,3,512]{2,1,0:T(4,128)S(1)}, f32[4,64,512]{2,1,0:T(8,128)S(1)}, f32[4,3,512]{2,1,0:T(4,128)S(1)}, /*index=5*/f...) while((s32[]{:T(128)}, f32[]{:T(128)}, ...), condition=%wide.region_11.12_spmd.clone, body=%wide.region_6.11_spmd.sunk.clone.sunk | while | flops 246597152 | bytes 9618793 | solution.py:81
  225.4 6.2 gather_fusion.15
  232.7 37.8 %while.58 = (s32[]{:T(128)}, f32[]{:T(128)}, f32[4,3,512]{2,1,0:T(4,128)S(1)}, f32[4,64,512]{2,1,0:T(8,128)S(1)}, f32[4,3,512]{2,1,0:T(4,128)S(1)}, /*index=5*/f...) while((s32[]{:T(128)}, f32[]{:T(128)}, ...), condition=%wide.region_17.18_spmd.clone, body=%wide.region_12.17_spmd.sunk.clone.sunk | while | flops 246597152 | bytes 9619301 | solution.py:81
  272.6 12.0 %scatter_custom_fusion.12 = f32[64,1536]{0,1:T(8,128)S(1)} fusion(s32[2048]{0:T(1024)S(1)} %bitcast.614, f32[2048,64]{1,0:T(8,128)} %copy.137, f32[]{:T(128)} %constant.151.clone.1), kind=kCustom, calls=%fused_computation.294 | custom fusion | flops 131072 | bytes 393728 | tf_op jit(solution)/shard_map/scatter-add | solution.py:178
  285.5 11.8 %scatter_custom_fusion.14 = f32[64,1536]{0,1:T(8,128)S(1)} fusion(s32[2048]{0:T(1024)} %bitcast.611, f32[2048,64]{1,0:T(8,128)S(1)} %copy.141, f32[]{:T(128)} %constant.151.clone.1), kind=kCustom, calls=%fused_computation.292 | custom fusion | flops 131072 | bytes 393728 | tf_op jit(solution)/shard_map/scatter-add | solution.py:181
  299.6 11.8 %scatter_custom_fusion.4 = f32[3,1536]{0,1:T(8,128)S(1)} fusion(s32[2048]{0:T(1024)} %bitcast.615, f32[2048,3]{1,0:T(8,128)S(1)} %copy.122, f32[]{:T(128)} %constant.151.clone.1), kind=kCustom, calls=%fused_computation.298 | custom fusion | flops 6144 | bytes 18944 | tf_op jit(solution)/shard_map/scatter-add | solution.py:177
  312.7 11.8 %scatter_custom_fusion.6 = f32[3,1536]{0,1:T(8,128)S(1)} fusion(s32[2048]{0:T(1024)} %bitcast.612, f32[2048,3]{1,0:T(8,128)S(1)} %copy.125, f32[]{:T(128)} %constant.151.clone.1), kind=kCustom, calls=%fused_computation.296 | custom fusion | flops 6144 | bytes 18944 | tf_op jit(solution)/shard_map/scatter-add | solution.py:180
  325.5 149.8 %while.56 = (s32[]{:T(128)}, f32[]{:T(128)}, f32[12,3,512]{2,1,0:T(4,128)S(1)}, f32[12,64,512]{2,1,0:T(8,128)}, f32[12,3,512]{2,1,0:T(4,128)S(1)}, /*index=5*/f3...) while((s32[]{:T(128)}, f32[]{:T(128)}, ...), condition=%wide.region_5.6_spmd, body=%wide.region_0.5_spmd.sunk | while | flops 246594080 | bytes 9616197 | solution.py:81
  476.9 2.3 copy.129
  480.8 2.2 copy.131
  483.0 2.2 copy.118
  485.2 2.2 copy.119
  487.4 33.7 %scatter_custom_fusion.8 = f32[64,2048]{0,1:T(8,128)S(1)} fusion(s32[6144]{0:T(1024)} %bitcast.608, f32[6144,64]{1,0:T(8,128)} %copy.129, f32[]{:T(128)} %constant.151.clone.1), kind=kCustom, calls=%fused_computation.288 | custom fusion | flops 393216 | bytes 524800 | tf_op jit(solution)/shard_map/scatter-add | solution.py:141
  521.2 33.9 %scatter_fusion.5 = f32[64,2048]{0,1:T(8,128)S(1)} fusion(f32[64,2048]{0,1:T(8,128)S(1)} %scatter_custom_fusion.8, s32[6144]{0:T(1024)S(1)} %bitcast.582, f32[6144,64]{1,0:T(8,128)} %copy.131), kind=kCustom, calls=%fused_computation.25 | custom fusion | flops 393216 | bytes 4743168 | tf_op jit(solution)/shard_map/scatter-add | solution.py:143
  555.1 33.7 %scatter_custom_fusion = f32[3,2048]{0,1:T(8,128)S(1)} fusion(s32[6144]{0:T(1024)} %bitcast.609, f32[6144,3]{1,0:T(8,128)} %copy.118, f32[]{:T(128)} %constant.151.clone.1), kind=kCustom, calls=%fused_computation.290 | custom fusion | flops 18432 | bytes 25088 | tf_op jit(solution)/shard_map/scatter-add | solution.py:136
  588.8 33.9 %scatter_fusion = f32[3,2048]{0,1:T(8,128)S(1)} fusion(f32[3,2048]{0,1:T(8,128)S(1)} %scatter_custom_fusion, s32[6144]{0:T(1024)S(1)} %bitcast.583, f32[6144,3]{1,0:T(8,128)} %copy.119), kind=kCustom, calls=%fused_computation.17 | custom fusion | flops 18432 | bytes 245760 | tf_op jit(solution)/shard_map/scatter-add | solution.py:136
  622.7 79.5 %psum.7 = f32[]{:T(128)} all-reduce(f32[]{:T(128)S(6)} %add.332), channel_id=1, replica_groups=mesh['gx'=32,'gy'=8] {'gx','gy'}, use_global_device_ids=true, to_apply=%region_18.19 | all-reduce | flops 1 | bytes 8 | tf_op jit(solution)/shard_map/psum | solution.py:185
  706.3 2.4 copy.135
  710.8 2.2 copy.121
  713.0 11.9 %scatter_fusion.6 = f32[64,2048]{0,1:T(8,128)S(1)} fusion(f32[64,2048]{0,1:T(8,128)S(1)} %scatter_fusion.5, s32[2048]{0:T(1024)S(1)} %bitcast.596, f32[2048,64]{1,0:T(8,128)S(1)} %copy.133), kind=kCustom, calls=%fused_computation.26 | custom fusion | flops 131072 | bytes 1581056 | tf_op jit(solution)/shard_map/scatter-add | solution.py:160
  724.9 12.2 %scatter_fusion.7 = f32[64,2048]{0,1:T(8,128)S(1)} fusion(f32[64,2048]{0,1:T(8,128)S(1)} %scatter_fusion.6, s32[2048]{0:T(1024)} %bitcast.599, f32[2048,64]{1,0:T(8,128)} %copy.135), kind=kCustom, calls=%fused_computation.27 | custom fusion | flops 131072 | bytes 1581056 | tf_op jit(solution)/shard_map/scatter-add | solution.py:176
  737.1 12.2 %scatter_fusion.1 = f32[3,2048]{0,1:T(8,128)S(1)} fusion(f32[3,2048]{0,1:T(8,128)S(1)} %scatter_fusion, s32[2048]{0:T(1024)S(1)} %bitcast.597, f32[2048,3]{1,0:T(8,128)} %copy.120), kind=kCustom, calls=%fused_computation.18 | custom fusion | flops 6144 | bytes 81920 | tf_op jit(solution)/shard_map/scatter-add | solution.py:159
  749.4 12.2 %scatter_fusion.2 = f32[3,2048]{0,1:T(8,128)S(1)} fusion(f32[3,2048]{0,1:T(8,128)S(1)} %scatter_fusion.1, s32[2048]{0:T(1024)S(1)} %bitcast.600, f32[2048,3]{1,0:T(8,128)} %copy.121), kind=kCustom, calls=%fused_computation.19 | custom fusion | flops 6144 | bytes 81920 | tf_op jit(solution)/shard_map/scatter-add | solution.py:175
  765.2 9.1 %scatter_fusion.3 = f32[3,2048]{0,1:T(8,128)S(1)} fusion(f32[3,2048]{0,1:T(8,128)S(1)} %scatter_fusion.2, s32[1536]{0:T(1024)S(1)} %copy-done.27, f32[1536,3]{1,0:T(8,128)S(1)} %copy.124), kind=kCustom, calls=%fused_computation.21 | custom fusion | flops 4608 | bytes 61440 | tf_op jit(solution)/shard_map/scatter-add | solution.py:183
  774.4 9.7 %scatter_fusion.4 = f32[3,2048]{0,1:T(8,128)S(1)} fusion(f32[3,2048]{0,1:T(8,128)S(1)} %scatter_fusion.3, s32[1536]{0:T(1024)S(1)} %copy-done.24, f32[1536,3]{1,0:T(8,128)} %copy.127), kind=kCustom, calls=%fused_computation.23 | custom fusion | flops 4608 | bytes 61440 | tf_op jit(solution)/shard_map/scatter-add | solution.py:183
  787.7 9.1 %scatter_fusion.8 = f32[64,2048]{0,1:T(8,128)S(1)} fusion(f32[64,2048]{0,1:T(8,128)S(1)} %scatter_fusion.7, s32[1536]{0:T(1024)S(1)} %copy-done.28, f32[1536,64]{1,0:T(8,128)S(1)} %copy.139), kind=kCustom, calls=%fused_computation.29 | custom fusion | flops 98304 | bytes 1185792 | tf_op jit(solution)/shard_map/scatter-add | solution.py:184
  796.9 9.1 %scatter_fusion.9 = f32[64,2048]{0,1:T(8,128)S(1)} fusion(f32[64,2048]{0,1:T(8,128)S(1)} %scatter_fusion.8, s32[1536]{0:T(1024)S(1)} %copy-done.25, f32[1536,64]{1,0:T(8,128)S(1)} %copy.143), kind=kCustom, calls=%fused_computation.31 | custom fusion | flops 98304 | bytes 1185792 | tf_op jit(solution)/shard_map/scatter-add | solution.py:184
  (554 shorter events, 251.8 us)
Async XLA Ops:
  0.6 8.2 %copy-start.12 = (bf16[64,2048]{1,0:T(8,128)(2,1)S(1)}, bf16[64,2048]{1,0:T(8,128)(2,1)}, u32[]{:S(2)}) copy-start(bf16[64,2048]{1,0:T(8,128)(2,1)} %param.24) | copy-start | bytes 786436
  2.6 2.9 copy-start.23
  5.5 157.8 %collective-permute-start = (f32[3,1536]{1,0:T(4,128)S(1)}, f32[3,1536]{1,0:T(4,128)}, u32[]{:S(2)}, u32[]{:S(2)}) collective-permute-start(f32[3,1536]{1,0:T(4,128)S(1)} %copy.99), channel_id=1, source_target_pairs={{0,248},{8,0},{16,8},{24,16},{32,24},{40,32},{48,40},{56,48},{64,5... | collective-permute-start | bytes 55304 | tf_op jit(solution)/shard_map/ppermute | solution.py:16
  13.2 16.9 %copy-start.32 = (s32[4,6144]{1,0:T(4,128)S(1)}, s32[4,6144]{1,0:T(4,128)}, u32[]{:S(2)}) copy-start(s32[4,6144]{1,0:T(4,128)} %param.26) | copy-start | bytes 294916
  13.2 17.1 %copy-start.36 = (s32[4,2048]{1,0:T(4,128)S(1)}, s32[4,2048]{1,0:T(4,128)}, u32[]{:S(2)}) copy-start(s32[4,2048]{1,0:T(4,128)} %param.27) | copy-start | bytes 98308
  13.2 17.2 %copy-start.37 = (s32[4,2048]{1,0:T(4,128)S(1)}, s32[4,2048]{1,0:T(4,128)}, u32[]{:S(2)}) copy-start(s32[4,2048]{1,0:T(4,128)} %param.28) | copy-start | bytes 98308
  13.2 170.5 %collective-permute-start.1 = (bf16[64,1536]{0,1:T(8,128)(2,1)}, bf16[64,1536]{0,1:T(8,128)(2,1)S(1)}, u32[]{:S(2)}, u32[]{:S(2)}) collective-permute-start(bf16[64,1536]{0,1:T(8,128)(2,1)} %bitcast.50), channel_id=1, source_target_pairs={{0,248},{8,0},{16,8},{24,16},{32,24},{40,32},{48,40},{56,48},{64,5... | collective-permute-start | bytes 589832 | tf_op jit(solution)/shard_map/ppermute | solution.py:16
  19.4 11.3 %copy-start.40 = (s32[1,3]{1,0:T(1,128)S(1)}, s32[1,3]{1,0:T(1,128)}, u32[]{:S(2)}) copy-start(s32[1,3]{1,0:T(1,128)} %param.29) | copy-start | bytes 40
  22.9 150.6 %collective-permute-start.2 = (f32[3,1536]{1,0:T(4,128)}, f32[3,1536]{1,0:T(4,128)}, u32[]{:S(2)}, u32[]{:S(2)}) collective-permute-start(f32[3,1536]{1,0:T(4,128)} %copy.109), channel_id=1, source_target_pairs={{0,7},{1,0},{2,1},{3,2},{4,3},{5,4},{6,5},{7,6},{8,15},{9,8},{10,9... | collective-permute-start | bytes 55304 | tf_op jit(solution)/shard_map/ppermute | solution.py:16
  29.5 195.8 %collective-permute-start.3 = (bf16[64,1536]{0,1:T(8,128)(2,1)}, bf16[64,1536]{0,1:T(8,128)(2,1)S(1)}, u32[]{:S(2)}, u32[]{:S(2)}) collective-permute-start(bf16[64,1536]{0,1:T(8,128)(2,1)} %bitcast.70), channel_id=1, source_target_pairs={{0,7},{1,0},{2,1},{3,2},{4,3},{5,4},{6,5},{7,6},{8,15},{9,8},{10,9... | collective-permute-start | bytes 589832 | tf_op jit(solution)/shard_map/ppermute | solution.py:16
  30.2 47.3 %copy-start.33 = (s32[6144,1]{0,1:T(1,128)}, s32[6144,1]{0,1:T(1,128)S(1)}, u32[]{:S(2)}) copy-start(s32[6144,1]{0,1:T(1,128)S(1)} %get-tuple-element.669) | copy-start | bytes 73732
  30.4 47.1 %copy-start.13 = (s32[2048,1]{0,1:T(1,128)}, s32[2048,1]{0,1:T(1,128)S(1)}, u32[]{:S(2)}) copy-start(s32[2048,1]{0,1:T(1,128)S(1)} %get-tuple-element.673) | copy-start | bytes 24580
  30.4 242.2 %copy-start.39 = (s32[2048,1]{0,1:T(1,128)}, s32[2048,1]{0,1:T(1,128)S(1)}, u32[]{:S(2)}) copy-start(s32[2048,1]{0,1:T(1,128)S(1)} %get-tuple-element.674) | copy-start | bytes 24580
  30.5 46.9 %copy-start.15 = (s32[2048,1]{0,1:T(1,128)}, s32[2048,1]{0,1:T(1,128)S(1)}, u32[]{:S(2)}) copy-start(s32[2048,1]{0,1:T(1,128)S(1)} %get-tuple-element.671) | copy-start | bytes 24580
  30.5 46.9 %copy-start.38 = (s32[2048,1]{0,1:T(1,128)}, s32[2048,1]{0,1:T(1,128)S(1)}, u32[]{:S(2)}) copy-start(s32[2048,1]{0,1:T(1,128)S(1)} %get-tuple-element.672) | copy-start | bytes 24580
  152.7 3.1 copy-start.2
  157.2 3.7 copy-start.6
  159.7 3.3 copy-start.5
  183.6 6.6 copy-start
  183.6 6.6 copy-start.1
  183.6 6.6 copy-start.7
  183.6 6.6 copy-start.8
  183.7 6.6 copy-start.9
  183.7 6.6 copy-start.29
  183.7 6.6 copy-start.35
  183.7 6.6 copy-start.41
  225.3 6.4 copy-start.17
  225.4 6.4 copy-start.18
  225.4 7.4 copy-start.34
  270.6 14.0 %copy-start.3 = (f32[4,64,512]{2,1,0:T(8,128)}, f32[4,64,512]{2,1,0:T(8,128)S(1)}, u32[]{:S(2)}) copy-start(f32[4,64,512]{2,1,0:T(8,128)S(1)} %get-tuple-element.358) | copy-start | bytes 1572868
  270.6 14.0 %copy-start.20 = (f32[4,3,512]{2,1,0:T(4,128)}, f32[4,3,512]{2,1,0:T(4,128)S(1)}, u32[]{:S(2)}) copy-start(f32[4,3,512]{2,1,0:T(4,128)S(1)} %get-tuple-element.352) | copy-start | bytes 73732
  271.2 14.0 %copy-start.4 = (f32[4,64,512]{2,1,0:T(8,128)S(1)}, f32[4,64,512]{2,1,0:T(8,128)}, u32[]{:S(2)}) copy-start(f32[4,64,512]{2,1,0:T(8,128)} %get-tuple-element.360) | copy-start | bytes 1572868
  284.9 500.3 %collective-permute-start.6 = (f32[64,1536]{1,0:T(8,128)S(1)}, f32[64,1536]{1,0:T(8,128)}, u32[]{:S(2)}, u32[]{:S(2)}) collective-permute-start(f32[64,1536]{1,0:T(8,128)S(1)} %copy.138), channel_id=1, source_target_pairs={{0,8},{8,16},{16,24},{24,32},{32,40},{40,48},{48,56},{56,64},{64,7... | collective-permute-start | bytes 1179656 | tf_op jit(solution)/shard_map/ppermute | solution.py:16
  285.2 14.0 %copy-start.19 = (f32[4,3,512]{2,1,0:T(4,128)S(1)}, f32[4,3,512]{2,1,0:T(4,128)}, u32[]{:S(2)}) copy-start(f32[4,3,512]{2,1,0:T(4,128)} %copy-done.18) | copy-start | bytes 73732
  298.3 14.0 %copy-start.22 = (f32[4,3,512]{2,1,0:T(4,128)S(1)}, f32[4,3,512]{2,1,0:T(4,128)}, u32[]{:S(2)}) copy-start(f32[4,3,512]{2,1,0:T(4,128)} %copy-done.21) | copy-start | bytes 73732
  298.3 488.1 %collective-permute-start.7 = (f32[64,1536]{1,0:T(8,128)}, f32[64,1536]{1,0:T(8,128)}, u32[]{:S(2)}, u32[]{:S(2)}) collective-permute-start(f32[64,1536]{1,0:T(8,128)} %copy.142), channel_id=1, source_target_pairs={{0,1},{1,2},{2,3},{3,4},{4,5},{5,6},{6,7},{7,0},{8,9},{9,10},{10,1... | collective-permute-start | bytes 1179656 | tf_op jit(solution)/shard_map/ppermute | solution.py:16
  311.4 14.1 %copy-start.30 = (f32[12,3,512]{2,1,0:T(4,128)S(1)}, f32[12,3,512]{2,1,0:T(4,128)}, u32[]{:S(2)}) copy-start(f32[12,3,512]{2,1,0:T(4,128)} %custom-call.32) | copy-start | bytes 221188
  311.4 14.1 %copy-start.31 = (f32[12,3,512]{2,1,0:T(4,128)S(1)}, f32[12,3,512]{2,1,0:T(4,128)}, u32[]{:S(2)}) copy-start(f32[12,3,512]{2,1,0:T(4,128)} %custom-call.34) | copy-start | bytes 221188
  311.4 14.1 %copy-start.43 = (bf16[256,64]{0,1:T(8,128)(2,1)S(1)}, bf16[256,64]{0,1:T(8,128)(2,1)}, u32[]{:S(2)}) copy-start(bf16[256,64]{0,1:T(8,128)(2,1)} %copy-done.42) | copy-start | bytes 98308
  312.3 450.0 %collective-permute-start.4 = (f32[3,1536]{1,0:T(4,128)}, f32[3,1536]{1,0:T(4,128)}, u32[]{:S(2)}, u32[]{:S(2)}) collective-permute-start(f32[3,1536]{1,0:T(4,128)} %copy.123), channel_id=1, source_target_pairs={{0,8},{8,16},{16,24},{24,32},{32,40},{40,48},{48,56},{56,64},{64,7... | collective-permute-start | bytes 55304 | tf_op jit(solution)/shard_map/ppermute | solution.py:16
  325.3 438.0 %collective-permute-start.5 = (f32[3,1536]{1,0:T(4,128)}, f32[3,1536]{1,0:T(4,128)}, u32[]{:S(2)}, u32[]{:S(2)}) collective-permute-start(f32[3,1536]{1,0:T(4,128)} %copy.126), channel_id=1, source_target_pairs={{0,1},{1,2},{2,3},{3,4},{4,5},{5,6},{6,7},{7,0},{8,9},{9,10},{10,1... | collective-permute-start | bytes 55304 | tf_op jit(solution)/shard_map/ppermute | solution.py:16
  485.2 35.9 %copy-start.11 = (s32[6144,1]{0,1:T(1,128)S(1)}, s32[6144,1]{0,1:T(1,128)}, u32[]{:S(2)}) copy-start(s32[6144,1]{0,1:T(1,128)} %copy-done.10) | copy-start | bytes 73732
  706.3 6.7 copy-start.14
  724.9 24.5 %copy-start.16 = (s32[2048,1]{0,1:T(1,128)S(1)}, s32[2048,1]{0,1:T(1,128)}, u32[]{:S(2)}) copy-start(s32[2048,1]{0,1:T(1,128)} %copy-done.15) | copy-start | bytes 24580
  737.1 28.1 %copy-start.27 = (s32[1536]{0:T(1024)S(1)}, s32[1536]{0:T(1024)}, u32[]{:S(2)}) copy-start(s32[1536]{0:T(1024)} %copy-done.26) | copy-start | bytes 18436
  737.1 37.3 %copy-start.24 = (s32[1536]{0:T(1024)S(1)}, s32[1536]{0:T(1024)}, u32[]{:S(2)}) copy-start(s32[1536]{0:T(1024)} %copy-done.23) | copy-start | bytes 18436
  784.2 3.5 copy-start.28
  787.7 9.2 %copy-start.25 = (s32[1536]{0:T(1024)S(1)}, s32[1536]{0:T(1024)}, u32[]{:S(2)}) copy-start(s32[1536]{0:T(1024)} %copy-done.23) | copy-start | bytes 18436
  (4 other events, 6.1 us)
where the time goes:
time: 820 us; the launch traced here: 808 us
  other arithmetic  304 us (37%)
  local copies, waits for them, and re-layouts  235 us (29%)
  matrix products  158 us (19%)
  blocking collectives  79.5 us (10%)
  loops' own time  14.5 us (2%)
  starting transfers between devices  14.1 us (2%)
    psum x1, blocking collectives, on_device(): total = lax.psum(energy_loc + energy_x + energy_y, ('gx', 'gy'))  79.5 us
    scatter-add x2, other arithmetic, on_device(): jnp.zeros((3, atoms), jnp.float32).at[:, source].add(grads[0]).at[:, target]  67.6 us
    scatter-add x2, other arithmetic, on_device(): grad_feat = jnp.zeros((width, atoms), jnp.float32).at[:, source].add(grad...  67.6 us
    dot_general x40, matrix products, pair_energy(): jnp.dot(w_hidden.T, hidden, preferred_element_type=jnp.float32)  60 us
    dot_general x40, matrix products, pair_energy(): jnp.dot(w_dst.T, dst_feat.astype(jnp.bfloat16), preferred_element_type=jn...  29.7 us
    dot_general x40, matrix products, pair_energy(): jnp.dot(w_src.T, src_feat.astype(jnp.bfloat16), preferred_element_type=jn...  27 us
    reshape x18, local copies, waits for them, and re-layouts, from_blocks(): return jnp.moveaxis(array, 0, 1).reshape(array.shape[1], -1)  25.3 us
    gather x1, local copies, waits for them, and re-layouts, on_device(): features[:, target]  22.1 us
  transfers between devices with their start and end apart: 8, of which 0 were waited for; matrix products, arithmetic and copies ran while one was open for 76% of the time, Pallas kernels for 0%

commit v1 on v0

v1 whole, which is shorter than its diff:
```python
import functools
import math

import jax
import jax.numpy as jnp
from jax import lax
from jax.experimental import pallas as pl
from jax.experimental.pallas import tpu as pltpu
from jax.sharding import PartitionSpec as P

CUTOFF = 6.0
EDGE = 6.0
SOFT = 0.1
BLK = 512
LO = 256
ROWS = 80
F32 = jnp.float32
BF16 = jnp.bfloat16


def shifted(array, axis, by):
    length = lax.axis_size(axis)
    return lax.ppermute(array, axis, [(i, (i + by) % length) for i in range(length)])


def silu_parts(x):
    sig = 0.5 * jnp.tanh(0.5 * x) + 0.5
    y = x * sig
    return y, sig + y * (1.0 - sig)


def sin_cos_pi(y):
    whole = jnp.floor(y + 0.5)
    t = (y - whole) * math.pi
    odd = whole - 2.0 * jnp.floor(whole * 0.5)
    sign = 1.0 - 2.0 * odd
    t2 = t * t
    s = -1.0 / 39916800.0
    for c in (1.0 / 362880.0, -1.0 / 5040.0, 1.0 / 120.0, -1.0 / 6.0, 1.0):
        s = s * t2 + c
    c_ = 1.0 / 479001600.0
    for c in (-1.0 / 3628800.0, 1.0 / 40320.0, -1.0 / 720.0, 1.0 / 24.0, -0.5, 1.0):
        c_ = c_ * t2 + c
    return s * t * sign, c_ * sign


def lane_lookup(table, index):
    chunks = table.shape[1] // 128
    parts = []
    for g in range(index.shape[1] // 128):
        ix = index[:, g * 128 : (g + 1) * 128]
        lane = jnp.broadcast_to(ix & 127, (8, 128))
        row = jnp.broadcast_to(ix >> 7, (8, 128))
        val = jnp.take_along_axis(table[:, 0:128], lane, axis=1, mode="promise_in_bounds")
        for c in range(1, chunks):
            got = jnp.take_along_axis(
                table[:, c * 128 : (c + 1) * 128], lane, axis=1, mode="promise_in_bounds"
            )
            val = jnp.where(row == c, got, val)
        parts.append(val)
    return jnp.concatenate(parts, axis=1)


def one_hot(index):
    low = (index & (LO - 1)).astype(F32)
    rows = lax.broadcasted_iota(jnp.int32, (LO, index.shape[1]), 0).astype(F32)
    return jnp.where(rows == low, 1.0, 0.0).astype(BF16)


def fill_tables(features_ref, positions_ref, table, place):
    atoms = features_ref.shape[1]
    width = features_ref.shape[0]
    for h in range(atoms // LO):
        table[h * width : (h + 1) * width, :] = features_ref[:, h * LO : (h + 1) * LO]
    place[...] = jnp.zeros_like(place)
    place[0:3, :] = positions_ref[...]


def fill_weights(w_rbf, w_src, w_dst, species_src, species_dst, w_hidden, w_latent, w_energy, wt, wb, wht, vec):
    stack = jnp.concatenate(
        [
            w_src[...].astype(F32),
            w_dst[...].astype(F32),
            w_rbf[...].astype(F32),
            species_src[...].astype(F32),
            species_dst[...].astype(F32),
        ],
        axis=0,
    )
    wb[...] = stack.astype(BF16)
    wt[...] = stack.T.astype(BF16)
    wht[...] = w_hidden[...].astype(F32).T.astype(BF16)
    score = jnp.sum(w_latent[...].astype(F32) * w_energy[...], axis=1, keepdims=True)
    vec[...] = jnp.broadcast_to(score, vec.shape)


def pick(table, hot, index):
    width = 64
    got = jnp.dot(table, hot, preferred_element_type=F32)
    hi = index >> 8
    out = got[0:width]
    for h in range(1, table.shape[0] // width):
        out = jnp.where(hi == h, got[h * width : (h + 1) * width], out)
    return out


def spread(values, index, count):
    hi = index >> 8
    return jnp.concatenate(
        [jnp.where(hi == h, values, 0.0).astype(BF16) for h in range(count)], axis=0
    )


def scatter_product(wide, hot):
    return lax.dot_general(wide, hot, (((1,), (1,)), ((), ())), preferred_element_type=F32)


def pair_block(src, dst, kind_src, kind_dst, live, offset, table_i, place_i, table_j, place_j, weights):
    wt, wb, wht, w_hidden, vec = weights
    width = src.shape[1]
    ids = lax.broadcasted_iota(jnp.int32, (8, width), 0)
    ids_f = ids.astype(F32)
    at = lane_lookup(place_j[...], dst)
    if offset is not None:
        at = at + jnp.where(ids == offset, EDGE, 0.0)
    diff = at - lane_lookup(place_i[...], src)
    r = jnp.sqrt(jnp.sum(diff * diff, axis=0, keepdims=True) + SOFT)
    inv = 1.0 / r
    order = ids_f + 1.0
    sine, cosine = sin_cos_pi(order * (r * (1.0 / CUTOFF)))
    basis = sine * inv
    slope = (order * (math.pi / CUTOFF) * cosine - basis) * inv
    kinds = jnp.where(ids < 4, kind_src, kind_dst + 4)
    species = jnp.where(ids == kinds, 1.0, 0.0)
    hot_i = one_hot(src)
    hot_j = one_hot(dst)
    x = jnp.concatenate(
        [
            pick(table_i[...], hot_i, src).astype(BF16),
            pick(table_j[...], hot_j, dst).astype(BF16),
            jnp.concatenate([basis, species], axis=0).astype(BF16),
        ],
        axis=0,
    )
    pre = jnp.dot(wt[...], x, preferred_element_type=F32)
    hidden, slope_one = silu_parts(pre)
    pre_two = jnp.dot(wht[...], hidden.astype(BF16), preferred_element_type=F32)
    second, slope_two = silu_parts(pre_two)
    v = vec[...][:, 0:1]
    score = jnp.sum(second * v, axis=0, keepdims=True)
    back = jnp.dot(w_hidden[...], (slope_two * v).astype(BF16), preferred_element_type=F32)
    grad_x = jnp.dot(wb[...], (back * slope_one).astype(BF16), preferred_element_type=F32)
    ratio = jnp.minimum(r * (1.0 / CUTOFF), 1.0)
    rest = 1.0 - ratio * ratio
    envelope = rest * rest * live
    energy = envelope * score
    grad_x = grad_x * envelope
    grad_r = jnp.sum(grad_x[128:136] * slope, axis=0, keepdims=True)
    grad_r = grad_r + score * live * (rest * ratio * (-4.0 / CUTOFF))
    grad_d = diff * (grad_r * inv)
    coarse = grad_d.astype(BF16).astype(F32)
    fine = grad_d - coarse
    place = jnp.concatenate([coarse, fine], axis=0)
    grad_i = jnp.concatenate([grad_x[0:64], -place], axis=0)
    grad_j = jnp.concatenate([grad_x[64:128], place], axis=0)
    return energy, grad_i, grad_j, hot_i, hot_j


def unpack(acc, feat_ref, place_ref):
    width = feat_ref.shape[0]
    for h in range(acc.shape[0] // ROWS):
        cols = slice(h * LO, (h + 1) * LO)
        feat_ref[:, cols] = acc[h * ROWS : h * ROWS + width, :].astype(feat_ref.dtype)
        fine = acc[h * ROWS + width : h * ROWS + width + 8, :] + acc[h * ROWS + width + 8 : h * ROWS + width + 16, :]
        place_ref[:, cols] = fine[0:3]


def local_kernel(first, last_call, *refs):
    (counts, pairs, positions, features, acc_in, energy_in, w_rbf, w_src, w_dst, species_src, species_dst, w_hidden,
     w_latent, w_energy) = refs[:14]
    if last_call:
        feat_out, place_out, energy, table, place, wt, wb, wht, vec, acc = refs[14:]
    else:
        acc, energy, table, place, wt, wb, wht, vec = refs[14:]
    step = pl.program_id(0)
    spans = features.shape[1] // LO

    @pl.when(step == 0)
    def _():
        fill_tables(features, positions, table, place)
        fill_weights(w_rbf, w_src, w_dst, species_src, species_dst, w_hidden, w_latent, w_energy, wt, wb, wht, vec)
        acc[...] = acc_in[...]
        energy[...] = energy_in[...]

    base = (step + first) * BLK

    @pl.when(base < counts[0, 0])
    def _():
        src, dst = pairs[0:1, :], pairs[1:2, :]
        slot = base + lax.broadcasted_iota(jnp.int32, (1, BLK), 1)
        live = jnp.where(slot < counts[0, 0], 1.0, 0.0)
        e, grad_i, grad_j, hot_i, hot_j = pair_block(
            src, dst, pairs[2:3, :], pairs[3:4, :], live, None, table, place, table, place, (wt, wb, wht, w_hidden, vec)
        )
        energy[...] += e
        acc[...] += scatter_product(spread(grad_i, src, spans), hot_i) + scatter_product(spread(grad_j, dst, spans), hot_j)

    if last_call:

        @pl.when(step == pl.num_programs(0) - 1)
        def _():
            unpack(acc, feat_out, place_out)


def cross_kernel(blocks, *refs):
    (counts, pairs_x, pairs_y, positions, features, positions_x, features_x, list_x, positions_y, features_y, list_y,
     acc_in, energy_in, w_rbf, w_src, w_dst, species_src, species_dst, w_hidden, w_latent, w_energy) = refs[:21]
    acc, energy, feat_x, place_x, feat_y, place_y, table, place, table_n, place_n, slots, wt, wb, wht, vec, acc_n = refs[21:]
    step = pl.program_id(0)
    spans = features.shape[1] // LO

    @pl.when(step == 0)
    def _():
        fill_tables(features, positions, table, place)
        fill_weights(w_rbf, w_src, w_dst, species_src, species_dst, w_hidden, w_latent, w_energy, wt, wb, wht, vec)
        acc[...] = acc_in[...]
        energy[...] = energy_in[...]

    def side(axis, pairs, positions_n, features_n, list_n, feat_n, place_out):
        first = axis * blocks

        @pl.when(step == first)
        def _():
            fill_tables(features_n, positions_n, table_n, place_n)
            slots[...] = jnp.broadcast_to(list_n[axis : axis + 1, :], slots.shape)
            acc_n[...] = jnp.zeros_like(acc_n)

        base = (step - first) * BLK

        @pl.when((step >= first) & (step < first + blocks) & (base < counts[0, 1 + axis]))
        def _():
            src = pairs[0:1, :]
            dst = lane_lookup(slots[...], pairs[1:2, :])[0:1]
            slot = base + lax.broadcasted_iota(jnp.int32, (1, BLK), 1)
            live = jnp.where(slot < counts[0, 1 + axis], 1.0, 0.0)
            e, grad_i, grad_j, hot_i, hot_j = pair_block(
                src, dst, pairs[2:3, :], pairs[3:4, :], live, axis, table, place, table_n, place_n,
                (wt, wb, wht, w_hidden, vec),
            )
            energy[...] += e
            acc[...] += scatter_product(spread(grad_i, src, spans), hot_i)
            acc_n[...] += scatter_product(spread(grad_j, dst, spans), hot_j)

        @pl.when(step == first + blocks - 1)
        def _():
            unpack(acc_n, feat_n, place_out)

    side(0, pairs_x, positions_x, features_x, list_x, feat_x, place_x)
    side(1, pairs_y, positions_y, features_y, list_y, feat_y, place_y)


def whole(array):
    return pl.BlockSpec(array.shape, lambda i: (0,) * len(array.shape))


SMEM = pl.BlockSpec(memory_space=pltpu.SMEM)


def weight_scratch(hid):
    return [
        pltpu.VMEM((hid, 144), BF16),
        pltpu.VMEM((144, hid), BF16),
        pltpu.VMEM((hid, hid), BF16),
        pltpu.VMEM((hid, 128), F32),
    ]


def run_local(first, blocks, last_call, counts, pairs, positions, features, acc, energy, weights):
    width, atoms = features.shape
    rest = (positions, features, acc, energy) + weights
    if last_call:
        outs = [jax.ShapeDtypeStruct((width, atoms), F32), jax.ShapeDtypeStruct((3, atoms), F32), energy]
    else:
        outs = [acc, energy]
    scratch = [pltpu.VMEM((atoms // LO * width, LO), BF16), pltpu.VMEM((8, atoms), F32)] + weight_scratch(
        weights[0].shape[1]
    )
    if last_call:
        scratch.append(pltpu.VMEM(acc.shape, F32))
    return pl.pallas_call(
        functools.partial(local_kernel, first, last_call),
        grid=(blocks,),
        in_specs=[SMEM, pl.BlockSpec((4, BLK), lambda i: (0, i + first))] + [whole(a) for a in rest],
        out_specs=[whole(o) for o in outs],
        out_shape=[jax.ShapeDtypeStruct(o.shape, o.dtype) for o in outs],
        scratch_shapes=scratch,
        compiler_params=pltpu.CompilerParams(vmem_limit_bytes=50 * 1024 * 1024),
        cost_estimate=pl.CostEstimate(flops=blocks * 3000000000, bytes_accessed=2000000, transcendentals=0),
    )(counts, pairs, *rest)


def run_cross(counts, pairs_x, pairs_y, rest, width, atoms):
    blocks = pairs_x.shape[1] // BLK
    acc, energy = rest[8], rest[9]
    outs = [acc, energy] + [jax.ShapeDtypeStruct((width, atoms), BF16), jax.ShapeDtypeStruct((3, atoms), F32)] * 2
    hid = rest[10].shape[1]
    table = pltpu.VMEM((atoms // LO * width, LO), BF16)
    place = pltpu.VMEM((8, atoms), F32)
    return pl.pallas_call(
        functools.partial(cross_kernel, blocks),
        grid=(2 * blocks,),
        in_specs=[
            SMEM,
            pl.BlockSpec((4, BLK), lambda i: (0, jnp.minimum(i, blocks - 1))),
            pl.BlockSpec((4, BLK), lambda i: (0, jnp.maximum(i - blocks, 0))),
        ]
        + [whole(a) for a in rest],
        out_specs=[whole(o) for o in outs],
        out_shape=[jax.ShapeDtypeStruct(o.shape, o.dtype) for o in outs],
        scratch_shapes=[table, place, table, place, pltpu.VMEM((8, rest[4].shape[1]), jnp.int32)]
        + weight_scratch(hid)
        + [pltpu.VMEM(acc.shape, F32)],
        compiler_params=pltpu.CompilerParams(vmem_limit_bytes=50 * 1024 * 1024),
        cost_estimate=pl.CostEstimate(flops=2 * blocks * 3000000000, bytes_accessed=2000000, transcendentals=0),
    )(counts, pairs_x, pairs_y, *rest)


EARLY = 4


def on_device(
    positions, features, halo_lists, local_pairs, cross_x, cross_y, pair_counts,
    w_rbf, w_src, w_dst, species_src, species_dst, w_hidden, w_latent, w_energy,
):
    width, atoms = features.shape
    weights = (w_rbf, w_src, w_dst, species_src, species_dst, w_hidden, w_latent, w_energy.reshape(1, -1))
    got_x = tuple(shifted(a, "gx", -1) for a in (positions, features, halo_lists))
    got_y = tuple(shifted(a, "gy", -1) for a in (positions, features, halo_lists))
    acc = jnp.zeros((atoms // LO * ROWS, LO), F32)
    energy = jnp.zeros((1, BLK), F32)
    acc, energy = run_local(0, EARLY, False, pair_counts, local_pairs, positions, features, acc, energy, weights)
    acc, energy, feat_x, place_x, feat_y, place_y = run_cross(
        pair_counts, cross_x, cross_y, (positions, features) + got_x + got_y + (acc, energy) + weights, width, atoms
    )
    back_x = (shifted(feat_x, "gx", 1), shifted(place_x, "gx", 1))
    back_y = (shifted(feat_y, "gy", 1), shifted(place_y, "gy", 1))
    late = local_pairs.shape[1] // BLK - EARLY
    feat, place, energy = run_local(
        EARLY, late, True, pair_counts, local_pairs, positions, features, acc, energy, weights
    )
    total = lax.psum(jnp.sum(energy), ("gx", "gy"))
    atoms_all = atoms * lax.axis_size("gx") * lax.axis_size("gy")
    feat = feat + back_x[0].astype(F32) + back_y[0].astype(F32)
    place = place + back_x[1] + back_y[1]
    return (total / atoms_all).reshape(1), -place, feat


def solution(mesh):
    split = P(None, ("gx", "gy"))
    return jax.shard_map(
        on_device,
        mesh=mesh,
        in_specs=(split,) * 6 + (P(("gx", "gy"), None),) + (P(),) * 8,
        out_specs=(P(), split, split),
        check_vma=False,
    )
```

time: 820 us -> 145 us (0.18); the launches traced: 808 us -> 144 us
  other arithmetic: 304 us -> 2.12 us
  local copies, waits for them, and re-layouts: 235 us -> 1.86 us
  matrix products: 158 us -> 0 us
  Pallas kernels: 0 us -> 17.5 us
  loops' own time: 14.5 us -> 0 us
  starting transfers between devices: 14.1 us -> 24.7 us
  waiting for transfers between devices: 0.02 us -> 9.71 us
    scatter-add x16 -> x0, other arithmetic: 268 us -> none  [the longest x2 67.6 us: on_device(): jnp.zeros((3, atoms), jnp.float32).at[:, source].add(grads[0]).at[:, target]]
    dot_general x240 -> x0, matrix products: 158 us -> none  [the longest x40 60 us: pair_energy(): jnp.dot(w_hidden.T, hidden, preferred_element_type=jnp.float32)]
    gather x18 -> x0, local copies, waits for them, and re-layouts: 158 us -> none  [the longest x1 22.1 us: on_device(): features[:, target]]
    reshape x30 -> x0, local copies, waits for them, and re-layouts: 41.1 us -> none  [the longest x18 25.3 us: from_blocks(): return jnp.moveaxis(array, 0, 1).reshape(array.shape[1], -1)]
    dynamic_slice x40 -> x0, local copies, waits for them, and re-layouts: 17.9 us -> none  [run_edges(): lax.scan(visit, jnp.zeros((), jnp.float32), tuple((to_blocks(item) for it...]
    pallas_call x0 -> x3, Pallas kernels: none -> 17.5 us  [the longest x2 12.6 us: run_local(): pl.pallas_call(functools.partial(local_kernel, first, last_call), grid=(b...]
    another operation x3 -> x0, loops' own time: 14.5 us -> none  [run_edges(): lax.scan(visit, jnp.zeros((), jnp.float32), tuple((to_blocks(item) for it...]
    mul x40 -> x0, other arithmetic: 12.9 us -> none  [the longest x20 12.8 us: pair_energy(): radius = jnp.sqrt(jnp.sum(displace * displace, axis=0) + softening)]
  transfers between devices with their start and end apart: 8 -> 10, of which waited for: 0 -> 2; matrix products, arithmetic and copies ran while one was open for 76% -> 1% of each run, Pallas kernels for 0% -> 9%
where the time goes in v1:
time: 145 us; the launch traced here: 144 us
  blocking collectives  85.8 us (59%)
  starting transfers between devices  24.7 us (17%)
  Pallas kernels  17.5 us (12%)
  waiting for transfers between devices  9.71 us (7%)
  between operations  2.66 us (2%)
  other arithmetic  2.12 us (1%)
  local copies, waits for them, and re-layouts  1.86 us (1%)
    psum x1, blocking collectives, on_device(): total = lax.psum(jnp.sum(energy), ('gx', 'gy'))  85.8 us
    ppermute x10, starting transfers between devices, shifted(): lax.ppermute(array, axis, [(i, (i + by) % length) for i in range(length)])  24.7 us
    pallas_call x2, Pallas kernels, run_local(): pl.pallas_call(functools.partial(local_kernel, first, last_call), grid=(b...  12.6 us
    ppermute x10, waiting for transfers between devices, shifted(): lax.ppermute(array, axis, [(i, (i + by) % length) for i in range(length)])  9.71 us
    pallas_call x1, Pallas kernels, run_cross(): pl.pallas_call(functools.partial(cross_kernel, blocks), grid=(2 * blocks,...  4.93 us
  transfers between devices with their start and end apart: 10, of which 2 were waited for; matrix products, arithmetic and copies ran while one was open for 1% of the time, Pallas kernels for 9%

profile of v1, /device:TPU:1, one launch (start us, length us, event | category | flops | bytes accessed | tf_op | source)
XLA Modules:
  0.0 144.3 jit_solution(17713272572901328547)
XLA Ops:
  0.6 4.4 %collective-permute-start.5 = (s32[2,1536]{1,0:T(2,128)}, s32[2,1536]{1,0:T(2,128)S(1)}, u32[]{:S(2)}, u32[]{:S(2)}) collective-permute-start(s32[2,1536]{1,0:T(2,128)} %param.17), channel_id=1, source_target_pairs={{0,7},{1,0},{2,1},{3,2},{4,3},{5,4},{6,5},{7,6},{8,15},{9,8},{10,9... | collective-permute-start | bytes 36872 | tf_op jit(solution)/shard_map/ppermute | solution.py:23
  5.0 1.0 collective-permute-start.2
  6.0 0.5 collective-permute-start.3
  6.5 7.0 %collective-permute-start = (f32[3,2048]{1,0:T(4,128)}, f32[3,2048]{1,0:T(4,128)S(1)}, u32[]{:S(2)}, u32[]{:S(2)}) collective-permute-start(f32[3,2048]{1,0:T(4,128)} %refs_2_.5), channel_id=1, source_target_pairs={{0,248},{8,0},{16,8},{24,16},{32,24},{40,32},{48,40},{56,48},{64,5... | collective-permute-start | bytes 73736 | tf_op jit(solution)/shard_map/ppermute | solution.py:23
  13.6 0.3 collective-permute-start.4
  13.8 0.9 copy.18.refs_12_.refs_19_
  14.7 0.0 collective-permute-done.5.refs_10_
  14.7 1.1 collective-permute-start.1
  15.8 0.0 copy-start.5
  15.8 0.0 copy-start.6
  15.8 0.0 copy-start.7
  15.9 0.0 copy-start.8
  15.9 0.0 copy-start.9
  15.9 0.0 copy-start.10
  15.9 0.0 copy-start.11
  15.9 0.0 copy-start.12
  16.0 0.8 copy-done
  16.8 0.0 copy-done.1
  16.8 0.1 copy-done.2
  16.9 0.0 copy-done.8
  16.9 0.0 copy-done.9
  16.9 0.0 copy-done.10
  16.9 0.0 copy-done.11
  16.9 0.0 copy-done.12
  16.9 0.0 copy-start.3
  16.9 0.0 copy-start.4
  16.9 8.0 %shard_map.166 = (f32[640,256]{1,0:T(8,128)S(1)}, f32[1,512]{1,0:T(1,128)S(1)}) custom-call(s32[1,3]{1,0:T(1,128)S(1)} %copy-done.11, s32[4,6144]{1,0:T(4,128)S(1)} %copy-done.2, f32[3,2048]{1,0:T(4,128)S(1)} %copy-done.5, bf16[64,2048]{1,0:T(8,128)(2,1)S(1)} %copy-done, f32[640,256]{1,0:T(8,128)S(1)} %broadcast_in_dim.6.refs_4_, ...), custom_call_target="tpu_custom_call" | custom-call | flops 12000000000 | bytes 2000000 | tf_op jit(solution)/shard_map/pallas_call | solution.py:290
  24.9 0.0 collective-permute-done.2.refs_7_
  24.9 0.0 collective-permute-done.3.refs_8_
  24.9 0.0 collective-permute-done.refs_5_
  24.9 0.0 collective-permute-done.4.refs_9_
  24.9 0.0 collective-permute-done.1.refs_6_
  24.9 0.0 copy-done.3
  25.0 0.0 copy-done.4
  25.0 4.9 %shard_map.167 = (f32[640,256]{1,0:T(8,128)S(1)}, f32[1,512]{1,0:T(1,128)S(1)}, bf16[64,2048]{1,0:T(8,128)(2,1)S(1)}, f32[3,2048]{1,0:T(4,128)S(1)}, bf16[64,204...) custom-call(s32[1,3]{1,0:T(1,128)S(1)} %copy-done.11, s32[4,2048]{1,0:T(4,128)S(1)} %copy-done.3, s32[4,2048]{1,0:T(4,128)S(1)} %copy-done.4, ...), custom_call_target="tpu_custom_call" | custom-call | flops 24000000000 | bytes 2000000 | tf_op jit(solution)/shard_map/pallas_call | solution.py:309
  29.9 0.8 collective-permute-start.6
  30.7 6.5 %collective-permute-start.7 = (f32[3,2048]{1,0:T(4,128)S(1)}, f32[3,2048]{1,0:T(4,128)S(1)}, u32[]{:S(2)}, u32[]{:S(2)}) collective-permute-start(f32[3,2048]{1,0:T(4,128)S(1)} %get-tuple-element.21), channel_id=1, source_target_pairs={{0,1},{1,2},{2,3},{3,4},{4,5},{5,6},{6,7},{7,0},{8,9},{9,10},{10,1... | collective-permute-start | bytes 73736 | tf_op jit(solution)/shard_map/ppermute | solution.py:23
  37.2 4.6 %shard_map.168 = (f32[64,2048]{1,0:T(8,128)S(1)}, f32[3,2048]{1,0:T(4,128)S(1)}, f32[1,512]{1,0:T(1,128)S(1)}) custom-call(s32[1,3]{1,0:T(1,128)S(1)} %copy-done.11, s32[4,6144]{1,0:T(4,128)S(1)} %copy-done.2, f32[3,2048]{1,0:T(4,128)S(1)} %copy-done.5, bf16[64,2048]{1,0:T(8,128)(2,1)S(1)} %copy-done, f32[640,256]{1,0:T(8,128)S(1)} %get-tuple-element.16.refs_4_, ...), custom_call_target="tpu_custom_call" | custom-call | flops 24000000000 | bytes 2000000 | tf_op jit(solution)/shard_map/pallas_call | solution.py:290
  41.8 0.6 reduce_sum.9
  42.4 85.8 %psum.7 = f32[]{:T(128)} all-reduce(f32[]{:T(128)} %reduce_sum.9), channel_id=1, replica_groups=mesh['gx'=32,'gy'=8] {'gx','gy'}, use_global_device_ids=true, to_apply=%region_1.0 | all-reduce | flops 1 | bytes 8 | tf_op jit(solution)/shard_map/psum | solution.py:351
  128.2 2.3 %collective-permute-start.8 = (bf16[64,2048]{1,0:T(8,128)(2,1)S(1)}, bf16[64,2048]{1,0:T(8,128)(2,1)S(1)}, u32[]{:S(2)}, u32[]{:S(2)}) collective-permute-start(bf16[64,2048]{1,0:T(8,128)(2,1)S(1)} %get-tuple-element.23), channel_id=1, source_target_pairs={{0,8},{8,16},{16,24},{24,32},{32,40},{40,48},{48,56},{56,64},{64,7... | collective-permute-start | bytes 786440 | tf_op jit(solution)/shard_map/ppermute | solution.py:23
  130.5 0.8 collective-permute-start.9
  131.9 0.0 collective-permute-done.6
  131.9 0.0 collective-permute-done.7
  131.9 0.6 add_negate_fusion
  132.6 1.3 collective-permute-done.8
  133.8 8.4 %collective-permute-done.9 = bf16[64,2048]{1,0:T(8,128)(2,1)S(1)} collective-permute-done((bf16[64,2048]{1,0:T(8,128)(2,1)S(1)}, bf16[64,2048]{1,0:T(8,128)(2,1)S(1)}, u32[]{:S(2)}, u32[]{:S(2)}) %collective-permute-start.9) | collective-permute-done | bytes 262176 | tf_op jit(solution)/shard_map/ppermute | solution.py:23
  142.3 0.9 convert_add_fusion
  (8 shorter events, 0.1 us)
Async XLA Ops:
  0.6 14.1 %collective-permute-start.5 = (s32[2,1536]{1,0:T(2,128)}, s32[2,1536]{1,0:T(2,128)S(1)}, u32[]{:S(2)}, u32[]{:S(2)}) collective-permute-start(s32[2,1536]{1,0:T(2,128)} %param.17), channel_id=1, source_target_pairs={{0,7},{1,0},{2,1},{3,2},{4,3},{5,4},{6,5},{7,6},{8,15},{9,8},{10,9... | collective-permute-start | bytes 36872 | tf_op jit(solution)/shard_map/ppermute | solution.py:23
  5.0 19.9 %collective-permute-start.2 = (s32[2,1536]{1,0:T(2,128)}, s32[2,1536]{1,0:T(2,128)S(1)}, u32[]{:S(2)}, u32[]{:S(2)}) collective-permute-start(s32[2,1536]{1,0:T(2,128)} %param.17), channel_id=1, source_target_pairs={{0,248},{8,0},{16,8},{24,16},{32,24},{40,32},{48,40},{56,48},{64,5... | collective-permute-start | bytes 36872 | tf_op jit(solution)/shard_map/ppermute | solution.py:23
  6.0 18.9 %collective-permute-start.3 = (f32[3,2048]{1,0:T(4,128)}, f32[3,2048]{1,0:T(4,128)S(1)}, u32[]{:S(2)}, u32[]{:S(2)}) collective-permute-start(f32[3,2048]{1,0:T(4,128)} %refs_2_.5), channel_id=1, source_target_pairs={{0,7},{1,0},{2,1},{3,2},{4,3},{5,4},{6,5},{7,6},{8,15},{9,8},{10,9... | collective-permute-start | bytes 73736 | tf_op jit(solution)/shard_map/ppermute | solution.py:23
  6.5 18.4 %collective-permute-start = (f32[3,2048]{1,0:T(4,128)}, f32[3,2048]{1,0:T(4,128)S(1)}, u32[]{:S(2)}, u32[]{:S(2)}) collective-permute-start(f32[3,2048]{1,0:T(4,128)} %refs_2_.5), channel_id=1, source_target_pairs={{0,248},{8,0},{16,8},{24,16},{32,24},{40,32},{48,40},{56,48},{64,5... | collective-permute-start | bytes 73736 | tf_op jit(solution)/shard_map/ppermute | solution.py:23
  13.6 11.4 %collective-permute-start.4 = (bf16[64,2048]{1,0:T(8,128)(2,1)}, bf16[64,2048]{1,0:T(8,128)(2,1)S(1)}, u32[]{:S(2)}, u32[]{:S(2)}) collective-permute-start(bf16[64,2048]{1,0:T(8,128)(2,1)} %refs_3_.5), channel_id=1, source_target_pairs={{0,7},{1,0},{2,1},{3,2},{4,3},{5,4},{6,5},{7,6},{8,15},{9,8},{10,9... | collective-permute-start | bytes 786440 | tf_op jit(solution)/shard_map/ppermute | solution.py:23
  14.7 10.2 %collective-permute-start.1 = (bf16[64,2048]{1,0:T(8,128)(2,1)}, bf16[64,2048]{1,0:T(8,128)(2,1)S(1)}, u32[]{:S(2)}, u32[]{:S(2)}) collective-permute-start(bf16[64,2048]{1,0:T(8,128)(2,1)} %refs_3_.5), channel_id=1, source_target_pairs={{0,248},{8,0},{16,8},{24,16},{32,24},{40,32},{48,40},{56,48},{64,5... | collective-permute-start | bytes 786440 | tf_op jit(solution)/shard_map/ppermute | solution.py:23
  15.8 0.9 copy-start
  15.8 1.0 copy-start.1
  15.8 1.0 copy-start.2
  15.8 1.0 copy-start.5
  15.8 1.0 copy-start.6
  15.8 1.0 copy-start.7
  15.9 1.0 copy-start.8
  15.9 1.0 copy-start.9
  15.9 1.0 copy-start.10
  15.9 1.0 copy-start.11
  15.9 1.0 copy-start.12
  16.9 8.1 %copy-start.3 = (s32[4,2048]{1,0:T(4,128)S(1)}, s32[4,2048]{1,0:T(4,128)}, u32[]{:S(2)}) copy-start(s32[4,2048]{1,0:T(4,128)} %refs_1_.4) | copy-start | bytes 98308
  16.9 8.0 %copy-start.4 = (s32[4,2048]{1,0:T(4,128)S(1)}, s32[4,2048]{1,0:T(4,128)}, u32[]{:S(2)}) copy-start(s32[4,2048]{1,0:T(4,128)} %refs_2_.4) | copy-start | bytes 98308
  29.9 102.0 %collective-permute-start.6 = (f32[3,2048]{1,0:T(4,128)S(1)}, f32[3,2048]{1,0:T(4,128)S(1)}, u32[]{:S(2)}, u32[]{:S(2)}) collective-permute-start(f32[3,2048]{1,0:T(4,128)S(1)} %get-tuple-element.20), channel_id=1, source_target_pairs={{0,8},{8,16},{16,24},{24,32},{32,40},{40,48},{48,56},{56,64},{64,7... | collective-permute-start | bytes 73736 | tf_op jit(solution)/shard_map/ppermute | solution.py:23
  30.7 101.2 %collective-permute-start.7 = (f32[3,2048]{1,0:T(4,128)S(1)}, f32[3,2048]{1,0:T(4,128)S(1)}, u32[]{:S(2)}, u32[]{:S(2)}) collective-permute-start(f32[3,2048]{1,0:T(4,128)S(1)} %get-tuple-element.21), channel_id=1, source_target_pairs={{0,1},{1,2},{2,3},{3,4},{4,5},{5,6},{6,7},{7,0},{8,9},{9,10},{10,1... | collective-permute-start | bytes 73736 | tf_op jit(solution)/shard_map/ppermute | solution.py:23
  128.2 5.6 %collective-permute-start.8 = (bf16[64,2048]{1,0:T(8,128)(2,1)S(1)}, bf16[64,2048]{1,0:T(8,128)(2,1)S(1)}, u32[]{:S(2)}, u32[]{:S(2)}) collective-permute-start(bf16[64,2048]{1,0:T(8,128)(2,1)S(1)} %get-tuple-element.23), channel_id=1, source_target_pairs={{0,8},{8,16},{16,24},{24,32},{32,40},{40,48},{48,56},{56,64},{64,7... | collective-permute-start | bytes 786440 | tf_op jit(solution)/shard_map/ppermute | solution.py:23
  130.5 11.8 %collective-permute-start.9 = (bf16[64,2048]{1,0:T(8,128)(2,1)S(1)}, bf16[64,2048]{1,0:T(8,128)(2,1)S(1)}, u32[]{:S(2)}, u32[]{:S(2)}) collective-permute-start(bf16[64,2048]{1,0:T(8,128)(2,1)S(1)} %get-tuple-element.24), channel_id=1, source_target_pairs={{0,1},{1,2},{2,3},{3,4},{4,5},{5,6},{6,7},{7,0},{8,9},{9,10},{10,1... | collective-permute-start | bytes 786440 | tf_op jit(solution)/shard_map/ppermute | solution.py:23

commit v2 on v1

v2 whole, which is shorter than its diff:
```python
import functools
import math

import jax
import jax.numpy as jnp
from jax import lax
from jax.experimental import pallas as pl
from jax.experimental.pallas import tpu as pltpu
from jax.sharding import PartitionSpec as P

CUTOFF = 6.0
EDGE = 6.0
SOFT = 0.1
BLK = 512
LO = 256
ROWS = 80
F32 = jnp.float32
BF16 = jnp.bfloat16


def silu_parts(x):
    sig = 0.5 * jnp.tanh(0.5 * x) + 0.5
    y = x * sig
    return y, sig + y * (1.0 - sig)


def sin_cos_pi(y):
    whole = jnp.floor(y + 0.5)
    t = (y - whole) * math.pi
    odd = whole - 2.0 * jnp.floor(whole * 0.5)
    sign = 1.0 - 2.0 * odd
    t2 = t * t
    s = -1.0 / 39916800.0
    for c in (1.0 / 362880.0, -1.0 / 5040.0, 1.0 / 120.0, -1.0 / 6.0, 1.0):
        s = s * t2 + c
    c_ = 1.0 / 479001600.0
    for c in (-1.0 / 3628800.0, 1.0 / 40320.0, -1.0 / 720.0, 1.0 / 24.0, -0.5, 1.0):
        c_ = c_ * t2 + c
    return s * t * sign, c_ * sign


def lane_lookup(table, index):
    chunks = table.shape[1] // 128
    parts = []
    for g in range(index.shape[1] // 128):
        ix = index[:, g * 128 : (g + 1) * 128]
        lane = jnp.broadcast_to(ix & 127, (8, 128))
        row = jnp.broadcast_to(ix >> 7, (8, 128))
        val = jnp.take_along_axis(table[:, 0:128], lane, axis=1, mode="promise_in_bounds")
        for c in range(1, chunks):
            got = jnp.take_along_axis(
                table[:, c * 128 : (c + 1) * 128], lane, axis=1, mode="promise_in_bounds"
            )
            val = jnp.where(row == c, got, val)
        parts.append(val)
    return jnp.concatenate(parts, axis=1)


def one_hot(index):
    low = (index & (LO - 1)).astype(F32)
    rows = lax.broadcasted_iota(jnp.int32, (LO, index.shape[1]), 0).astype(F32)
    return jnp.where(rows == low, 1.0, 0.0).astype(BF16)


def fill_weights(w_rbf, w_src, w_dst, species_src, species_dst, w_hidden, w_latent, w_energy, wt, wb, wht, vec):
    stack = jnp.concatenate(
        [
            w_src[...].astype(F32),
            w_dst[...].astype(F32),
            w_rbf[...].astype(F32),
            species_src[...].astype(F32),
            species_dst[...].astype(F32),
        ],
        axis=0,
    )
    wb[...] = stack.astype(BF16)
    wt[...] = stack.T.astype(BF16)
    wht[...] = w_hidden[...].astype(F32).T.astype(BF16)
    score = jnp.sum(w_latent[...].astype(F32) * w_energy[...], axis=1, keepdims=True)
    vec[...] = jnp.broadcast_to(score, vec.shape)


def pick(table, hot, index):
    width = 64
    got = jnp.dot(table, hot, preferred_element_type=F32)
    hi = index >> 8
    out = got[0:width]
    for h in range(1, table.shape[0] // width):
        out = jnp.where(hi == h, got[h * width : (h + 1) * width], out)
    return out


def spread(values, index, count):
    hi = index >> 8
    return jnp.concatenate(
        [jnp.where(hi == h, values, 0.0).astype(BF16) for h in range(count)], axis=0
    )


def scatter_product(wide, hot):
    return lax.dot_general(wide, hot, (((1,), (1,)), ((), ())), preferred_element_type=F32)


def pair_block(src, dst, kind_src, kind_dst, live, offset, table_i, place_i, table_j, place_j, weights):
    wt, wb, wht, w_hidden, vec = weights
    width = src.shape[1]
    ids = lax.broadcasted_iota(jnp.int32, (8, width), 0)
    ids_f = ids.astype(F32)
    at = lane_lookup(place_j[...], dst)
    if offset is not None:
        at = at + jnp.where(ids == offset, EDGE, 0.0)
    diff = jnp.where(ids < 3, at - lane_lookup(place_i[...], src), 0.0)
    r = jnp.sqrt(jnp.sum(diff * diff, axis=0, keepdims=True) + SOFT)
    inv = 1.0 / r
    order = ids_f + 1.0
    sine, cosine = sin_cos_pi(order * (r * (1.0 / CUTOFF)))
    basis = sine * inv
    slope = (order * (math.pi / CUTOFF) * cosine - basis) * inv
    kinds = jnp.where(ids < 4, kind_src, kind_dst + 4)
    species = jnp.where(ids == kinds, 1.0, 0.0)
    hot_i = one_hot(src)
    hot_j = one_hot(dst)
    x = jnp.concatenate(
        [
            pick(table_i[...], hot_i, src).astype(BF16),
            pick(table_j[...], hot_j, dst).astype(BF16),
            jnp.concatenate([basis, species], axis=0).astype(BF16),
        ],
        axis=0,
    )
    pre = jnp.dot(wt[...], x, preferred_element_type=F32)
    hidden, slope_one = silu_parts(pre)
    pre_two = jnp.dot(wht[...], hidden.astype(BF16), preferred_element_type=F32)
    second, slope_two = silu_parts(pre_two)
    v = vec[...][:, 0:1]
    score = jnp.sum(second * v, axis=0, keepdims=True)
    back = jnp.dot(w_hidden[...], (slope_two * v).astype(BF16), preferred_element_type=F32)
    grad_x = jnp.dot(wb[...], (back * slope_one).astype(BF16), preferred_element_type=F32)
    ratio = jnp.minimum(r * (1.0 / CUTOFF), 1.0)
    rest = 1.0 - ratio * ratio
    envelope = rest * rest * live
    energy = envelope * score
    grad_x = grad_x * envelope
    grad_r = jnp.sum(grad_x[128:136] * slope, axis=0, keepdims=True)
    grad_r = grad_r + score * live * (rest * ratio * (-4.0 / CUTOFF))
    grad_d = diff * (grad_r * inv)
    coarse = grad_d.astype(BF16).astype(F32)
    fine = grad_d - coarse
    place = jnp.concatenate([coarse, fine], axis=0)
    grad_i = jnp.concatenate([grad_x[0:64], -place], axis=0)
    grad_j = jnp.concatenate([grad_x[64:128], place], axis=0)
    return energy, grad_i, grad_j, hot_i, hot_j


def compact(acc, message):
    for h in range(acc.shape[0] // ROWS):
        top = h * ROWS
        place = acc[top + 64 : top + 72, :] + acc[top + 72 : top + 80, :]
        coarse = place.astype(BF16).astype(F32)
        rows = jnp.concatenate([acc[top : top + 64, :], coarse, place - coarse], axis=0)
        message[top : top + ROWS, :] = rows.astype(BF16)


def kernel(
    sizes, early, counts, local_pairs, pairs_x, pairs_y, positions, features, lists, w_rbf, w_src, w_dst, species_src,
    species_dst, w_hidden, w_latent, w_energy, energy_out, forces, feat_out, table, place, tables_n, places_n, wt, wb,
    wht, vec, acc, acc_n, message, message_n, energy, energy_one, energy_two, got_one, got_two, send_sem, recv_sem,
    send_one, recv_one, send_two, recv_two,
):
    n_gx, n_gy = sizes
    gx, gy = lax.axis_index("gx"), lax.axis_index("gy")
    width, atoms = features.shape
    spans = atoms // LO

    def peer(axis, by):
        if axis == 0:
            return (lax.rem(gx + by + n_gx, n_gx), gy)
        return (gx, lax.rem(gy + by + n_gy, n_gy))

    barrier = pltpu.get_barrier_semaphore()

    def greet(axis):
        def visit(by, carry):
            pl.semaphore_signal(barrier, inc=1, device_id=peer(axis, by), device_id_type=pl.DeviceIdType.MESH)
            return carry

        lax.fori_loop(1, sizes[axis], visit, 0)

    greet(0)
    greet(1)
    for h in range(spans):
        table[h * width : (h + 1) * width, :] = features[:, h * LO : (h + 1) * LO]
    place[...] = jnp.zeros_like(place)
    place[0:3, :] = positions[...]
    place[3:5, 0 : lists.shape[1]] = lists[...].astype(F32)
    pl.semaphore_wait(barrier, n_gx + n_gy - 2)

    def lend(axis, part, source, target, by):
        return pltpu.make_async_remote_copy(
            src_ref=source,
            dst_ref=target,
            send_sem=send_sem.at[axis, part],
            recv_sem=recv_sem.at[axis, part],
            device_id=peer(axis, by),
            device_id_type=pl.DeviceIdType.MESH,
        )

    halos = [
        (lend(axis, 0, table, tables_n.at[axis], -1), lend(axis, 1, place, places_n.at[axis], -1)) for axis in (0, 1)
    ]
    for pair in halos:
        for copy in pair:
            copy.start()
    fill_weights(w_rbf, w_src, w_dst, species_src, species_dst, w_hidden, w_latent, w_energy, wt, wb, wht, vec)
    acc[...] = jnp.zeros_like(acc)
    acc_n[...] = jnp.zeros_like(acc_n)
    energy[...] = jnp.zeros_like(energy)
    weights = (wt, wb, wht, w_hidden, vec)

    def columns(pairs, step, limit):
        base = pl.multiple_of(step * BLK, BLK)
        block = pairs[:, pl.ds(base, BLK)]
        slot = base + lax.broadcasted_iota(jnp.int32, (1, BLK), 1)
        live = jnp.where(slot < limit, 1.0, 0.0)
        return block[0:1], block[1:2], block[2:3], block[3:4], live

    def local_step(step, carry):
        src, dst, kind_src, kind_dst, live = columns(local_pairs, step, counts[0, 0])
        e, grad_i, grad_j, hot_i, hot_j = pair_block(
            src, dst, kind_src, kind_dst, live, None, table, place, table, place, weights
        )
        energy[...] += e
        acc[...] += scatter_product(spread(grad_i, src, spans), hot_i) + scatter_product(
            spread(grad_j, dst, spans), hot_j
        )
        return carry

    def cross_step(axis, pairs, step, carry):
        src, slots, kind_src, kind_dst, live = columns(pairs, step, counts[0, 1 + axis])
        place_n = places_n.at[axis]
        dst = lane_lookup(place_n[:, 0 : lists.shape[1]], slots)[3 + axis : 4 + axis].astype(jnp.int32)
        e, grad_i, grad_j, hot_i, hot_j = pair_block(
            src, dst, kind_src, kind_dst, live, axis, table, place, tables_n.at[axis], place_n, weights
        )
        energy[...] += e
        acc[...] += scatter_product(spread(grad_i, src, spans), hot_i)
        acc_n[axis] += scatter_product(spread(grad_j, dst, spans), hot_j)
        return carry

    lax.fori_loop(0, early, local_step, 0)
    returns = []
    for axis, pairs in ((0, pairs_x), (1, pairs_y)):
        for copy in halos[axis]:
            copy.wait_recv()
        lax.fori_loop(0, pairs.shape[1] // BLK, functools.partial(cross_step, axis, pairs), 0)
        compact(acc_n.at[axis], message.at[axis])
        back = lend(axis, 2, message.at[axis], message_n.at[axis], 1)
        back.start()
        returns.append(back)
    lax.fori_loop(early, local_pairs.shape[1] // BLK, local_step, 0)

    def exchange(axis, value, source, target, send, recv):
        count = sizes[axis]

        def copy_of(by):
            return pltpu.make_async_remote_copy(
                src_ref=source,
                dst_ref=target.at[by],
                send_sem=send.at[by],
                recv_sem=recv.at[by],
                device_id=peer(axis, by),
                device_id_type=pl.DeviceIdType.MESH,
            )

        def start(by, carry):
            copy_of(by).start()
            return carry

        def wait(by, carry):
            copy_of(by).wait()
            return carry

        source[...] = value
        lax.fori_loop(1, count, start, 0)
        return lambda: lax.fori_loop(1, count, wait, 0)

    total = jnp.broadcast_to(jnp.sum(energy[...], axis=1, keepdims=True), energy_one.shape)
    wait_one = exchange(1, total, energy_one, got_one, send_one, recv_one)
    wait_one()
    total = total + jnp.sum(got_one[1:n_gy], axis=0)
    wait_two = exchange(0, total, energy_two, got_two, send_two, recv_two)
    for pair in halos:
        for copy in pair:
            copy.wait_send()
    for back in returns:
        back.wait()
    for h in range(spans):
        top = h * ROWS
        cols = slice(h * LO, (h + 1) * LO)
        rows = acc[top : top + ROWS, :]
        for axis in (0, 1):
            rows = rows + message_n[axis, top : top + ROWS, :].astype(F32)
        feat_out[:, cols] = rows[0:width]
        forces[:, cols] = -(rows[width : width + 8] + rows[width + 8 : width + 16])[0:3]
    wait_two()
    total = total + jnp.sum(got_two[1:n_gx], axis=0)
    energy_out[...] = total[0:1, 0:1] / (atoms * n_gx * n_gy)


EARLY = 5


def on_device(
    positions, features, halo_lists, local_pairs, cross_x, cross_y, pair_counts,
    w_rbf, w_src, w_dst, species_src, species_dst, w_hidden, w_latent, w_energy,
):
    width, atoms = features.shape
    hid = w_hidden.shape[0]
    sizes = (lax.axis_size("gx"), lax.axis_size("gy"))
    spans = atoms // LO
    vmem = pl.BlockSpec(memory_space=pltpu.VMEM)
    dma = pltpu.SemaphoreType.DMA
    energy, forces, feat = pl.pallas_call(
        functools.partial(kernel, sizes, EARLY),
        in_specs=[pl.BlockSpec(memory_space=pltpu.SMEM)] + [vmem] * 14,
        out_specs=[vmem] * 3,
        out_shape=[
            jax.ShapeDtypeStruct((1, 1), F32),
            jax.ShapeDtypeStruct((3, atoms), F32),
            jax.ShapeDtypeStruct((width, atoms), F32),
        ],
        scratch_shapes=[
            pltpu.VMEM((spans * width, LO), BF16),
            pltpu.VMEM((8, atoms), F32),
            pltpu.VMEM((2, spans * width, LO), BF16),
            pltpu.VMEM((2, 8, atoms), F32),
            pltpu.VMEM((hid, 144), BF16),
            pltpu.VMEM((144, hid), BF16),
            pltpu.VMEM((hid, hid), BF16),
            pltpu.VMEM((hid, 128), F32),
            pltpu.VMEM((spans * ROWS, LO), F32),
            pltpu.VMEM((2, spans * ROWS, LO), F32),
            pltpu.VMEM((2, spans * ROWS, LO), BF16),
            pltpu.VMEM((2, spans * ROWS, LO), BF16),
            pltpu.VMEM((1, BLK), F32),
            pltpu.VMEM((8, 128), F32),
            pltpu.VMEM((8, 128), F32),
            pltpu.VMEM((sizes[1], 8, 128), F32),
            pltpu.VMEM((sizes[0], 8, 128), F32),
            dma((2, 3)),
            dma((2, 3)),
            dma((sizes[1],)),
            dma((sizes[1],)),
            dma((sizes[0],)),
            dma((sizes[0],)),
        ],
        compiler_params=pltpu.CompilerParams(
            collective_id=0, has_side_effects=True, vmem_limit_bytes=56 * 1024 * 1024
        ),
        cost_estimate=pl.CostEstimate(flops=60000000000, bytes_accessed=4000000, transcendentals=0),
    )(
        pair_counts, local_pairs, cross_x, cross_y, positions, features, halo_lists,
        w_rbf, w_src, w_dst, species_src, species_dst, w_hidden, w_latent, w_energy.reshape(1, -1),
    )
    return energy.reshape(1), forces, feat


def solution(mesh):
    split = P(None, ("gx", "gy"))
    return jax.shard_map(
        on_device,
        mesh=mesh,
        in_specs=(split,) * 6 + (P(("gx", "gy"), None),) + (P(),) * 8,
        out_specs=(P(), split, split),
        check_vma=False,
    )
```

time: 145 us -> 67.3 us (0.46)
  blocking collectives: 85.8 us -> 0 us
  Pallas kernels: 17.5 us -> 59.8 us
  starting transfers between devices: 24.7 us -> 0 us
  waiting for transfers between devices: 9.71 us -> 0 us
  local copies, waits for them, and re-layouts: 1.86 us -> 4.74 us
  other arithmetic: 2.12 us -> 0 us
    psum x1 -> x0, blocking collectives: 85.8 us -> none  [on_device(): total = lax.psum(jnp.sum(energy), ('gx', 'gy'))]
    pallas_call x3 -> x1, Pallas kernels: 17.5 us -> 59.8 us  [on_device(): pl.pallas_call(functools.partial(kernel, sizes, EARLY), in_specs=[pl.Bloc...]
    ppermute x10 -> x0, starting transfers between devices: 24.7 us -> none  [shifted(): lax.ppermute(array, axis, [(i, (i + by) % length) for i in range(length)])]
    ppermute x10 -> x0, waiting for transfers between devices: 9.71 us -> none  [shifted(): lax.ppermute(array, axis, [(i, (i + by) % length) for i in range(length)])]
    unnamed x27 -> x3, local copies, waits for them, and re-layouts: 1.81 us -> 4.74 us
  transfers between devices with their start and end apart: 10 -> 0, of which waited for: 2 -> 0; matrix products, arithmetic and copies ran while one was open for 1% -> 0% of each run, Pallas kernels for 9% -> 0%
where the time goes in v2:
time: 67.3 us; the launch traced here: 67 us
  Pallas kernels  59.8 us (89%)
  local copies, waits for them, and re-layouts  4.74 us (7%)
  between operations  2.37 us (4%)
    pallas_call x1, Pallas kernels, on_device(): pl.pallas_call(functools.partial(kernel, sizes, EARLY), in_specs=[pl.Bloc...  59.8 us
    unnamed x3, local copies, waits for them, and re-layouts  4.74 us

profile of v2, /device:TPU:1, one launch (start us, length us, event | category | flops | bytes accessed | tf_op | source)
XLA Modules:
  0.0 67.0 jit_solution(5398007054179345464)
XLA Ops:
  0.6 1.5 %copy.18.w_latent = bf16[256,64]{1,0:T(8,128)(2,1)} copy(bf16[256,64]{0,1:T(8,128)(2,1)} %param.28) | data formatting | bytes 65536 | tf_op args[13]
  2.1 59.8 %shard_map.166 = (f32[1,1]{1,0:T(1,128)}, f32[3,2048]{1,0:T(4,128)}, f32[64,2048]{1,0:T(8,128)}) custom-call(s32[1,3]{1,0:T(1,128)} %counts.1, s32[4,6144]{1,0:T(4,128)} %local_pairs.1, s32[4,2048]{1,0:T(4,128)} %pairs_x.1, s32[4,2048]{1,0:T(4,128)} %pairs_y.1, f32[3,2048]{1,0:T(4,128)} %positions.1, bf16[64,2048]{1,0:T(8,128)(2,1)} %features.1, ...), custom_call_target="tpu_custom_call" | custom-call | flops 60000002048 | bytes 4000000 | tf_op jit(solution)/shard_map/pallas_call | solution.py:323
  62.6 1.4 %copy.23 = f32[3,2048]{1,0:T(4,128)} copy(f32[3,2048]{1,0:T(4,128)} %get-tuple-element.13) | data formatting | bytes 49152
  64.0 1.9 %copy.24 = f32[64,2048]{1,0:T(8,128)} copy(f32[64,2048]{1,0:T(8,128)} %get-tuple-element.14) | data formatting | bytes 1048576

commit v3 on v2

v3 whole, which is shorter than its diff:
```python
import functools
import math

import jax
import jax.numpy as jnp
from jax import lax
from jax.experimental import pallas as pl
from jax.experimental.pallas import tpu as pltpu
from jax.sharding import PartitionSpec as P

CUTOFF = 6.0
EDGE = 6.0
SOFT = 0.1
BLK = 1024
EARLY = 3
LO = 256
VMEM_LIMIT = 60 * 1024 * 1024
F32 = jnp.float32
BF16 = jnp.bfloat16
MESH = pl.DeviceIdType.MESH


def silu_parts(x):
    sig = 0.5 * jnp.tanh(0.5 * x) + 0.5
    y = x * sig
    return y, sig + y * (1.0 - sig)


def sin_cos_pi(y):
    whole = jnp.floor(y + 0.5)
    t = (y - whole) * math.pi
    odd = whole - 2.0 * jnp.floor(whole * 0.5)
    sign = 1.0 - 2.0 * odd
    t2 = t * t
    s = -1.0 / 39916800.0
    for c in (1.0 / 362880.0, -1.0 / 5040.0, 1.0 / 120.0, -1.0 / 6.0, 1.0):
        s = s * t2 + c
    c_ = 1.0 / 479001600.0
    for c in (-1.0 / 3628800.0, 1.0 / 40320.0, -1.0 / 720.0, 1.0 / 24.0, -0.5, 1.0):
        c_ = c_ * t2 + c
    return s * t * sign, c_ * sign


def lane_lookup(table, index):
    parts = []
    for g in range(index.shape[1] // 128):
        ix = index[:, g * 128 : (g + 1) * 128]
        lane = ix & 127
        chunk = ix >> 7
        val = None
        for c in range(table.shape[1] // 128):
            got = jnp.take_along_axis(
                table[:, c * 128 : (c + 1) * 128], lane, axis=1, mode="promise_in_bounds"
            )
            val = got if c == 0 else jnp.where(chunk == c, got, val)
        parts.append(val)
    return jnp.concatenate(parts, axis=1)


def one_hot(index):
    low = (index & (LO - 1)).astype(F32)
    rows = lax.broadcasted_iota(jnp.int32, (LO, index.shape[1]), 0).astype(F32)
    return jnp.where(rows == low, 1.0, 0.0).astype(BF16)


def pick(table, index, width):
    got = jnp.dot(table, one_hot(index), preferred_element_type=F32)
    hi = index >> 8
    out = got[0:width]
    for h in range(1, table.shape[0] // width):
        out = jnp.where(hi == h, got[h * width : (h + 1) * width], out)
    return out


def scatter_product(feat, place, index, spans):
    hi = index >> 8
    half = lax.broadcasted_iota(jnp.int32, place.shape, 0) >> 2
    parts = [jnp.where(hi == h, feat, 0.0).astype(BF16) for h in range(spans)]
    pairs = [jnp.where(hi == 2 * g + half, place, 0.0) for g in range(spans // 2)]
    parts.append(jnp.concatenate(pairs, axis=0).astype(BF16))
    wide = jnp.concatenate(parts, axis=0)
    return lax.dot_general(
        wide, one_hot(index), (((1,), (1,)), ((), ())), preferred_element_type=F32
    )


def fill_weights(refs, wt, wb, wht, vec):
    w_rbf, w_src, w_dst, species_src, species_dst, w_hidden, w_latent_t, w_energy = refs
    stack = jnp.concatenate(
        [a[...].astype(F32) for a in (w_src, w_dst, w_rbf, species_src, species_dst)], axis=0
    )
    wb[...] = stack.astype(BF16)
    wt[...] = stack.T.astype(BF16)
    wht[...] = w_hidden[...].astype(F32).T.astype(BF16)
    score = jnp.sum(w_latent_t[...].astype(F32).T * w_energy[...], axis=1, keepdims=True)
    vec[...] = jnp.broadcast_to(score, vec.shape)


def pair_block(first, second, kind_src, kind_dst, live, both, table_i, table_j, weights):
    wt, wb, wht, w_hidden, vec = weights
    width = first.shape[1]
    ids = lax.broadcasted_iota(jnp.int32, (8, width), 0)
    found = lane_lookup(both, jnp.where(ids < 4, first, second))
    target = found[7:8].astype(jnp.int32)
    diff = jnp.where(ids < 3, jnp.concatenate([found[4:8], found[0:4]], axis=0) - found, 0.0)
    r = jnp.sqrt(jnp.sum(diff * diff, axis=0, keepdims=True) + SOFT)
    inv = 1.0 / r
    order = ids.astype(F32) + 1.0
    sine, cosine = sin_cos_pi(order * (r * (1.0 / CUTOFF)))
    basis = sine * inv
    slope = (order * (math.pi / CUTOFF) * cosine - basis) * inv
    species = jnp.where(ids == jnp.where(ids < 4, kind_src, kind_dst + 4), 1.0, 0.0)
    feats = 64
    x = jnp.concatenate(
        [
            pick(table_i[...], first, feats).astype(BF16),
            pick(table_j[...], target, feats).astype(BF16),
            jnp.concatenate([basis, species], axis=0).astype(BF16),
        ],
        axis=0,
    )
    pre = jnp.dot(wt[...], x, preferred_element_type=F32)
    hidden, slope_one = silu_parts(pre)
    pre_two = jnp.dot(wht[...], hidden.astype(BF16), preferred_element_type=F32)
    top, slope_two = silu_parts(pre_two)
    v = vec[...][:, 0:1]
    score = jnp.sum(top * v, axis=0, keepdims=True)
    back = jnp.dot(w_hidden[...], (slope_two * v).astype(BF16), preferred_element_type=F32)
    grad_x = jnp.dot(wb[...], (back * slope_one).astype(BF16), preferred_element_type=F32)
    ratio = jnp.minimum(r * (1.0 / CUTOFF), 1.0)
    rest = 1.0 - ratio * ratio
    envelope = rest * rest * live
    grad_x = grad_x * envelope
    grad_r = jnp.sum(grad_x[2 * feats : 2 * feats + 8] * slope, axis=0, keepdims=True)
    grad_r = grad_r + score * live * (rest * ratio * (-4.0 / CUTOFF))
    grad_d = diff * (grad_r * inv)
    grad_d = grad_d + jnp.concatenate([grad_d[4:8], grad_d[0:4]], axis=0)
    return envelope * score, grad_x[0:feats], grad_x[feats : 2 * feats], grad_d, target


def kernel(
    sizes, counts, local_pairs, pairs_x, pairs_y, positions, features, lists, w_rbf, w_src, w_dst, species_src,
    species_dst, w_hidden, w_latent, w_energy, energy_out, sums_out, pairs, tables, lent, lent_n, both, wt, wb,
    wht, vec, acc_i, acc_j, message, message_n, hold_i, hold_j, hold_d, hold_ids, energy, energy_one, energy_two,
    got_one, got_two, send_sem, recv_sem, send_one, recv_one, send_two, recv_two,
):
    n_gx, n_gy = sizes
    gx, gy = lax.axis_index("gx"), lax.axis_index("gy")
    width, atoms = features.shape
    spans = atoms // LO
    halo = lists.shape[1]
    n_cross = pairs_x.shape[1] // BLK
    n_all = pairs.shape[1] // BLK
    start_x, start_y, start_late = EARLY, EARLY + n_cross, EARLY + 2 * n_cross

    def peer(axis, by):
        if axis == 0:
            return (lax.rem(gx + by + n_gx, n_gx), gy)
        return (gx, lax.rem(gy + by + n_gy, n_gy))

    barrier = pltpu.get_barrier_semaphore()
    for axis in (0, 1):

        def greet(by, carry):
            pl.semaphore_signal(barrier, inc=1, device_id=peer(axis, by), device_id_type=MESH)
            return carry

        lax.fori_loop(1, sizes[axis], greet, 0)

    early = EARLY * BLK
    pairs[:, 0:early] = local_pairs[:, 0:early]
    pairs[:, early : early + pairs_x.shape[1]] = pairs_x[...]
    pairs[:, early + pairs_x.shape[1] : start_late * BLK] = pairs_y[...]
    pairs[:, start_late * BLK :] = local_pairs[:, early:]
    for h in range(spans):
        tables[0, h * width : (h + 1) * width, :] = features[:, h * LO : (h + 1) * LO]
    place = positions[...]
    zero = jnp.zeros((1, atoms), F32)
    number = lax.broadcasted_iota(jnp.int32, (1, atoms), 1).astype(F32)
    both[0] = jnp.concatenate([place, zero, place, number], axis=0)
    for axis in (0, 1):
        picked = lane_lookup(both[0], jnp.broadcast_to(lists[axis : axis + 1, :], (8, halo)))
        lent[axis] = picked
    fill_weights(
        (w_rbf, w_src, w_dst, species_src, species_dst, w_hidden, w_latent, w_energy), wt, wb, wht, vec
    )
    acc_i[...] = jnp.zeros_like(acc_i)
    acc_j[...] = jnp.zeros_like(acc_j)
    energy[...] = jnp.zeros_like(energy)
    weights = (wt, wb, wht, w_hidden, vec)

    def lend(axis, part, source, target, by):
        return pltpu.make_async_remote_copy(
            src_ref=source,
            dst_ref=target,
            send_sem=send_sem.at[axis, part],
            recv_sem=recv_sem.at[axis, part],
            device_id=peer(axis, by),
            device_id_type=MESH,
        )

    halos = [
        (
            lend(axis, 0, tables.at[0], tables.at[axis + 1], -1),
            lend(axis, 1, lent.at[axis], lent_n.at[axis], -1),
        )
        for axis in (0, 1)
    ]
    returns = [lend(axis, 2, message.at[axis], message_n.at[axis], 1) for axis in (0, 1)]

    def side_of(step):
        cross = jnp.where(step < start_y, 1, 2)
        return jnp.where(step < start_x, 0, jnp.where(step < start_late, cross, 0))

    def network(step):
        side = side_of(step)
        skipped = jnp.where(
            side == 0, jnp.where(step < start_x, 0, 2 * n_cross), jnp.where(side == 1, start_x, start_y)
        )
        block = pairs[:, pl.ds(pl.multiple_of(step * BLK, BLK), BLK)]
        slot = (step - skipped) * BLK + lax.broadcasted_iota(jnp.int32, (1, BLK), 1)
        live = jnp.where(slot < counts[0, side], 1.0, 0.0)
        e, grad_i, grad_j, grad_d, target = pair_block(
            block[0:1], block[1:2], block[2:3], block[3:4], live, both[side], tables.at[0], tables.at[side], weights
        )
        energy[...] += e
        hold_i[...] = grad_i
        hold_j[...] = grad_j
        hold_d[...] = grad_d
        hold_ids[0:1, :] = block[0:1]
        hold_ids[1:2, :] = target

    def scatter(step):
        side = side_of(step)
        acc_i[...] += scatter_product(hold_i[...], -hold_d[...], hold_ids[0:1, :], spans)
        acc_j[side] += scatter_product(hold_j[...], hold_d[...], hold_ids[1:2, :], spans)

    network(0)
    pl.semaphore_wait(barrier, n_gx + n_gy - 2)
    for group in halos:
        for copy in group:
            copy.start()

    def visit(step, carry):
        for axis, begin in ((0, start_x), (1, start_y)):

            @pl.when(step == begin)
            def _():
                for copy in halos[axis]:
                    copy.wait_recv()
                ids = lax.broadcasted_iota(jnp.int32, (8, halo), 0)
                far = lent_n[axis] + jnp.where(ids == 4 + axis, EDGE, 0.0)
                both[axis + 1] = both[0]
                both[axis + 1, :, 0:halo] = jnp.where(ids < 4, both[0, :, 0:halo], far)

        scatter(step - 1)
        network(step)
        for axis, end in ((0, start_y), (1, start_late)):

            @pl.when(step == end)
            def _():
                message[axis] = acc_j[axis + 1].astype(BF16)
                returns[axis].start()

        return carry

    lax.fori_loop(1, n_all, visit, 0)

    def exchange(axis, value, source, target, send, recv):
        def copy_of(by):
            return pltpu.make_async_remote_copy(
                src_ref=source,
                dst_ref=target.at[by],
                send_sem=send.at[by],
                recv_sem=recv.at[by],
                device_id=peer(axis, by),
                device_id_type=MESH,
            )

        def start(by, carry):
            copy_of(by).start()
            return carry

        def wait(by, carry):
            copy_of(by).wait()
            return carry

        source[...] = value
        lax.fori_loop(1, sizes[axis], start, 0)
        return lambda: lax.fori_loop(1, sizes[axis], wait, 0)

    total = jnp.broadcast_to(jnp.sum(energy[...], axis=1, keepdims=True), energy_one.shape)
    wait_one = exchange(1, total, energy_one, got_one, send_one, recv_one)
    scatter(n_all - 1)
    wait_one()
    total = total + jnp.sum(got_one[1:n_gy], axis=0)
    wait_two = exchange(0, total, energy_two, got_two, send_two, recv_two)
    for group in halos:
        for copy in group:
            copy.wait_send()
    for back in returns:
        back.wait()
    sums_out[...] = acc_i[...] + acc_j[0] + message_n[0].astype(F32) + message_n[1].astype(F32)
    wait_two()
    total = total + jnp.sum(got_two[1:n_gx], axis=0)
    energy_out[...] = total[0:1, 0:1] / (atoms * n_gx * n_gy)


def finish(energy_in, sums, energy, forces, feat):
    width, atoms = feat.shape
    spans = atoms // LO
    energy[...] = energy_in[...]
    for h in range(spans):
        cols = slice(h * LO, (h + 1) * LO)
        rows = slice(h * width, (h + 1) * width)
        feat[:, cols] = sums[rows, :]
        top = spans * width + 4 * h
        forces[:, cols] = -sums[top : top + 3, :]


def on_device(
    positions, features, halo_lists, local_pairs, cross_x, cross_y, pair_counts,
    w_rbf, w_src, w_dst, species_src, species_dst, w_hidden, w_latent, w_energy,
):
    width, atoms = features.shape
    hid = w_hidden.shape[0]
    n_gx, n_gy = lax.axis_size("gx"), lax.axis_size("gy")
    spans = atoms // LO
    rows = spans * width + spans * 4
    halo = halo_lists.shape[1]
    slots = local_pairs.shape[1] + cross_x.shape[1] + cross_y.shape[1]
    vmem = pl.BlockSpec(memory_space=pltpu.VMEM)
    dma = pltpu.SemaphoreType.DMA
    sums = jax.ShapeDtypeStruct((rows, LO), F32)
    one = jax.ShapeDtypeStruct((1, 1), F32)
    partial = pl.pallas_call(
        functools.partial(kernel, (n_gx, n_gy)),
        in_specs=[pl.BlockSpec(memory_space=pltpu.SMEM)] + [vmem] * 14,
        out_specs=[vmem] * 2,
        out_shape=[one, sums],
        scratch_shapes=[
            pltpu.VMEM((4, slots), jnp.int32),
            pltpu.VMEM((3, spans * width, LO), BF16),
            pltpu.VMEM((2, 8, halo), F32),
            pltpu.VMEM((2, 8, halo), F32),
            pltpu.VMEM((3, 8, atoms), F32),
            pltpu.VMEM((hid, 144), BF16),
            pltpu.VMEM((144, hid), BF16),
            pltpu.VMEM((hid, hid), BF16),
            pltpu.VMEM((hid, 128), F32),
            pltpu.VMEM((rows, LO), F32),
            pltpu.VMEM((3, rows, LO), F32),
            pltpu.VMEM((2, rows, LO), BF16),
            pltpu.VMEM((2, rows, LO), BF16),
            pltpu.VMEM((width, BLK), F32),
            pltpu.VMEM((width, BLK), F32),
            pltpu.VMEM((8, BLK), F32),
            pltpu.VMEM((8, BLK), jnp.int32),
            pltpu.VMEM((1, BLK), F32),
            pltpu.VMEM((8, 128), F32),
            pltpu.VMEM((8, 128), F32),
            pltpu.VMEM((n_gy, 8, 128), F32),
            pltpu.VMEM((n_gx, 8, 128), F32),
            dma((2, 3)),
            dma((2, 3)),
            dma((n_gy,)),
            dma((n_gy,)),
            dma((n_gx,)),
            dma((n_gx,)),
        ],
        compiler_params=pltpu.CompilerParams(
            collective_id=0, has_side_effects=True, vmem_limit_bytes=VMEM_LIMIT
        ),
        cost_estimate=pl.CostEstimate(flops=30000000000, bytes_accessed=4000000, transcendentals=0),
    )(
        pair_counts, local_pairs, cross_x, cross_y, positions, features, halo_lists,
        w_rbf, w_src, w_dst, species_src, species_dst, w_hidden, w_latent.T, w_energy.reshape(1, -1),
    )
    energy, forces, feat = pl.pallas_call(
        finish,
        in_specs=[vmem] * 2,
        out_specs=[vmem] * 3,
        out_shape=[
            one,
            jax.ShapeDtypeStruct((3, atoms), F32),
            jax.ShapeDtypeStruct((width, atoms), F32),
        ],
        compiler_params=pltpu.CompilerParams(vmem_limit_bytes=VMEM_LIMIT),
        cost_estimate=pl.CostEstimate(flops=1000000, bytes_accessed=2000000, transcendentals=0),
    )(*partial)
    return energy.reshape(1), forces, feat


def solution(mesh):
    split = P(None, ("gx", "gy"))
    return jax.shard_map(
        on_device,
        mesh=mesh,
        in_specs=(split,) * 6 + (P(("gx", "gy"), None),) + (P(),) * 8,
        out_specs=(P(), split, split),
        check_vma=False,
    )
```

time: 67.3 us -> 54 us (0.80)
  Pallas kernels: 59.8 us -> 53.2 us
  local copies, waits for them, and re-layouts: 4.74 us -> 0 us
  between operations: 2.37 us -> 0.65 us
    pallas_call x1 -> x2, Pallas kernels: 59.8 us -> 53.2 us  [the longest x1 50.7 us: on_device(): pl.pallas_call(functools.partial(kernel, (n_gx, n_gy)), in_specs=[pl.Bloc...]
    unnamed x3 -> x0, local copies, waits for them, and re-layouts: 4.74 us -> none
where the time goes in v3:
time: 54 us; the launch traced here: 53.8 us
  Pallas kernels  53.2 us (99%)
  between operations  0.65 us (1%)
    pallas_call x1, Pallas kernels, on_device(): pl.pallas_call(functools.partial(kernel, (n_gx, n_gy)), in_specs=[pl.Bloc...  50.7 us
    pallas_call x1, Pallas kernels, on_device(): pl.pallas_call(finish, in_specs=[vmem] * 2, out_specs=[vmem] * 3, out_sha...  2.45 us

profile of v3, /device:TPU:1, one launch (start us, length us, event | category | flops | bytes accessed | tf_op | source)
XLA Modules:
  0.0 53.8 jit_solution(501167790821064479)
XLA Ops:
  0.6 50.7 %shard_map.166 = (f32[1,1]{1,0:T(1,128)}, f32[544,256]{1,0:T(8,128)}) custom-call(s32[1,3]{1,0:T(1,128)} %counts.1, s32[4,6144]{1,0:T(4,128)} %local_pairs.1, s32[4,2048]{1,0:T(4,128)} %pairs_x.1, s32[4,2048]{1,0:T(4,128)} %pairs_y.1, f32[3,2048]{1,0:T(4,128)} %positions.1, bf16[64,2048]{1,0:T(8,128)(2,1)} %features.1, s32[2,1536]{1,0:T(2,128)} %lists.1, ...), custom_call_target="tpu_custom_call" | custom-call | flops 30000001024 | bytes 4000000 | tf_op jit(solution)/shard_map/pallas_call | solution.py:336
  51.4 2.4 %shard_map.167 = (f32[1,1]{1,0:T(1,128)}, f32[3,2048]{1,0:T(4,128)}, f32[64,2048]{1,0:T(8,128)}) custom-call(f32[1,1]{1,0:T(1,128)} %get-tuple-element.8.energy_in, f32[544,256]{1,0:T(8,128)} %get-tuple-element.9.sums), custom_call_target="tpu_custom_call" | custom-call | flops 1000000 | bytes 2000000 | tf_op jit(solution)/shard_map/pallas_call | solution.py:379

commit v4 on v3

--- a/solution.py
+++ b/solution.py
@@ -12,7 +12,10 @@
 EDGE = 6.0
 SOFT = 0.1
 BLK = 1024
-EARLY = 3
+EARLY = 4
+PARTS = 1
+CHUNK = 1024
+DELAY = 1
 LO = 256
 VMEM_LIMIT = 60 * 1024 * 1024
 F32 = jnp.float32
@@ -99,9 +102,13 @@
 def pair_block(first, second, kind_src, kind_dst, live, both, table_i, table_j, weights):
     wt, wb, wht, w_hidden, vec = weights
     width = first.shape[1]
+    feats = 64
     ids = lax.broadcasted_iota(jnp.int32, (8, width), 0)
     found = lane_lookup(both, jnp.where(ids < 4, first, second))
     target = found[7:8].astype(jnp.int32)
+    yield None
+    x_i = pick(table_i[...], first, feats).astype(BF16)
+    yield None
     diff = jnp.where(ids < 3, jnp.concatenate([found[4:8], found[0:4]], axis=0) - found, 0.0)
     r = jnp.sqrt(jnp.sum(diff * diff, axis=0, keepdims=True) + SOFT)
     inv = 1.0 / r
@@ -110,23 +117,28 @@
     basis = sine * inv
     slope = (order * (math.pi / CUTOFF) * cosine - basis) * inv
     species = jnp.where(ids == jnp.where(ids < 4, kind_src, kind_dst + 4), 1.0, 0.0)
-    feats = 64
-    x = jnp.concatenate(
-        [
-            pick(table_i[...], first, feats).astype(BF16),
-            pick(table_j[...], target, feats).astype(BF16),
-            jnp.concatenate([basis, species], axis=0).astype(BF16),
-        ],
-        axis=0,
-    )
+    yield None
+    x_j = pick(table_j[...], target, feats).astype(BF16)
+    x = jnp.concatenate([x_i, x_j, jnp.concatenate([basis, species], axis=0).astype(BF16)], axis=0)
+    yield None
     pre = jnp.dot(wt[...], x, preferred_element_type=F32)
+    yield None
     hidden, slope_one = silu_parts(pre)
-    pre_two = jnp.dot(wht[...], hidden.astype(BF16), preferred_element_type=F32)
+    hidden = hidden.astype(BF16)
+    yield None
+    pre_two = jnp.dot(wht[...], hidden, preferred_element_type=F32)
+    yield None
     top, slope_two = silu_parts(pre_two)
     v = vec[...][:, 0:1]
     score = jnp.sum(top * v, axis=0, keepdims=True)
-    back = jnp.dot(w_hidden[...], (slope_two * v).astype(BF16), preferred_element_type=F32)
-    grad_x = jnp.dot(wb[...], (back * slope_one).astype(BF16), preferred_element_type=F32)
+    down = (slope_two * v).astype(BF16)
+    yield None
+    back = jnp.dot(w_hidden[...], down, preferred_element_type=F32)
+    yield None
+    down = (back * slope_one).astype(BF16)
+    yield None
+    grad_x = jnp.dot(wb[...], down, preferred_element_type=F32)
+    yield None
     ratio = jnp.minimum(r * (1.0 / CUTOFF), 1.0)
     rest = 1.0 - ratio * ratio
     envelope = rest * rest * live
@@ -135,7 +147,7 @@
     grad_r = grad_r + score * live * (rest * ratio * (-4.0 / CUTOFF))
     grad_d = diff * (grad_r * inv)
     grad_d = grad_d + jnp.concatenate([grad_d[4:8], grad_d[0:4]], axis=0)
-    return envelope * score, grad_x[0:feats], grad_x[feats : 2 * feats], grad_d, target
+    yield envelope * score, grad_x[0:feats], grad_x[feats : 2 * feats], grad_d, target
 
 
 def kernel(
@@ -212,34 +224,61 @@
         cross = jnp.where(step < start_y, 1, 2)
         return jnp.where(step < start_x, 0, jnp.where(step < start_late, cross, 0))
 
-    def network(step):
+    def network(step, part):
+        size = BLK // PARTS
         side = side_of(step)
         skipped = jnp.where(
             side == 0, jnp.where(step < start_x, 0, 2 * n_cross), jnp.where(side == 1, start_x, start_y)
         )
-        block = pairs[:, pl.ds(pl.multiple_of(step * BLK, BLK), BLK)]
-        slot = (step - skipped) * BLK + lax.broadcasted_iota(jnp.int32, (1, BLK), 1)
+        block = pairs[:, pl.ds(pl.multiple_of(step * BLK + part * size, size), size)]
+        slot = (step - skipped) * BLK + part * size + lax.broadcasted_iota(jnp.int32, (1, size), 1)
         live = jnp.where(slot < counts[0, side], 1.0, 0.0)
-        e, grad_i, grad_j, grad_d, target = pair_block(
+        for got in pair_block(
             block[0:1], block[1:2], block[2:3], block[3:4], live, both[side], tables.at[0], tables.at[side], weights
-        )
-        energy[...] += e
-        hold_i[...] = grad_i
-        hold_j[...] = grad_j
-        hold_d[...] = grad_d
-        hold_ids[0:1, :] = block[0:1]
-        hold_ids[1:2, :] = target
+        ):
+            if got is None:
+                yield
+        yield
+        cols = slice(part * size, (part + 1) * size)
+        energy[:, cols] += got[0]
+        hold_i[:, cols] = got[1]
+        hold_j[:, cols] = got[2]
+        hold_d[:, cols] = got[3]
+        hold_ids[0:1, cols] = block[0:1]
+        hold_ids[1:2, cols] = got[4]
 
     def scatter(step):
         side = side_of(step)
-        acc_i[...] += scatter_product(hold_i[...], -hold_d[...], hold_ids[0:1, :], spans)
-        acc_j[side] += scatter_product(hold_j[...], hold_d[...], hold_ids[1:2, :], spans)
-
-    network(0)
+        for c in range(BLK // CHUNK):
+            cols = slice(c * CHUNK, (c + 1) * CHUNK)
+            acc_i[...] += scatter_product(hold_i[:, cols], -hold_d[:, cols], hold_ids[0:1, cols], spans)
+            yield
+            acc_j[side] += scatter_product(hold_j[:, cols], hold_d[:, cols], hold_ids[1:2, cols], spans)
+            yield
+
+    def turn(old, new):
+        nets = [] if new is None else [network(new, part) for part in range(PARTS)]
+        flows = nets + ([] if old is None else [scatter(old)])
+        waits = [part * DELAY for part in range(len(nets))] + [0]
+        left = list(zip(flows, waits))
+        stages = 13
+        done = {id(f): 0 for f in flows}
+        for tick in range(100):
+            for flow, wait in list(left):
+                is_net = flow in nets
+                if tick < wait or (is_net and done[id(flow)] == stages - 1):
+                    continue
+                done[id(flow)] += 1
+                if next(flow, "end") == "end":
+                    left.remove((flow, wait))
+        for flow in nets:
+            next(flow, None)
+
     pl.semaphore_wait(barrier, n_gx + n_gy - 2)
     for group in halos:
         for copy in group:
             copy.start()
+    turn(None, 0)
 
     def visit(step, carry):
         for axis, begin in ((0, start_x), (1, start_y)):
@@ -253,8 +292,7 @@
                 both[axis + 1] = both[0]
                 both[axis + 1, :, 0:halo] = jnp.where(ids < 4, both[0, :, 0:halo], far)
 
-        scatter(step - 1)
-        network(step)
+        turn(step - 1, step)
         for axis, end in ((0, start_y), (1, start_late)):
 
             @pl.when(step == end)
@@ -291,7 +329,7 @@
 
     total = jnp.broadcast_to(jnp.sum(energy[...], axis=1, keepdims=True), energy_one.shape)
     wait_one = exchange(1, total, energy_one, got_one, send_one, recv_one)
-    scatter(n_all - 1)
+    turn(n_all - 1, None)
     wait_one()
     total = total + jnp.sum(got_one[1:n_gy], axis=0)
     wait_two = exchange(0, total, energy_two, got_two, send_two, recv_two)

time: 54 us -> 53.7 us (level)
  no operation moved by 1% of the time
where the time goes in v4:
time: 53.7 us; the launch traced here: 53.5 us
  Pallas kernels  52.9 us (99%)
  between operations  0.65 us (1%)
    pallas_call x1, Pallas kernels, on_device(): pl.pallas_call(functools.partial(kernel, (n_gx, n_gy)), in_specs=[pl.Bloc...  50.4 us
    pallas_call x1, Pallas kernels, on_device(): pl.pallas_call(finish, in_specs=[vmem] * 2, out_specs=[vmem] * 3, out_sha...  2.45 us

profile of v4, /device:TPU:1, one launch (start us, length us, event | category | flops | bytes accessed | tf_op | source)
XLA Modules:
  0.0 53.5 jit_solution(14274128654667594329)
XLA Ops:
  0.6 50.4 %shard_map.166 = (f32[1,1]{1,0:T(1,128)}, f32[544,256]{1,0:T(8,128)}) custom-call(s32[1,3]{1,0:T(1,128)} %counts.1, s32[4,6144]{1,0:T(4,128)} %local_pairs.1, s32[4,2048]{1,0:T(4,128)} %pairs_x.1, s32[4,2048]{1,0:T(4,128)} %pairs_y.1, f32[3,2048]{1,0:T(4,128)} %positions.1, bf16[64,2048]{1,0:T(8,128)(2,1)} %features.1, s32[2,1536]{1,0:T(2,128)} %lists.1, ...), custom_call_target="tpu_custom_call" | custom-call | flops 30000001024 | bytes 4000000 | tf_op jit(solution)/shard_map/pallas_call | solution.py:374
  51.1 2.4 %shard_map.167 = (f32[1,1]{1,0:T(1,128)}, f32[3,2048]{1,0:T(4,128)}, f32[64,2048]{1,0:T(8,128)}) custom-call(f32[1,1]{1,0:T(1,128)} %get-tuple-element.8.energy_in, f32[544,256]{1,0:T(8,128)} %get-tuple-element.9.sums), custom_call_target="tpu_custom_call" | custom-call | flops 1000000 | bytes 2000000 | tf_op jit(solution)/shard_map/pallas_call | solution.py:417

commit v5 on v3

--- a/solution.py
+++ b/solution.py
@@ -11,8 +11,7 @@
 CUTOFF = 6.0
 EDGE = 6.0
 SOFT = 0.1
-BLK = 1024
-EARLY = 3
+BLK = 2048
 LO = 256
 VMEM_LIMIT = 60 * 1024 * 1024
 F32 = jnp.float32
@@ -96,10 +95,10 @@
     vec[...] = jnp.broadcast_to(score, vec.shape)
 
 
-def pair_block(first, second, kind_src, kind_dst, live, both, table_i, table_j, weights):
-    wt, wb, wht, w_hidden, vec = weights
-    width = first.shape[1]
-    ids = lax.broadcasted_iota(jnp.int32, (8, width), 0)
+def forward(first, second, kind_src, kind_dst, live, both, table_i, table_j, weights):
+    wt, wht, vec = weights
+    feats = table_i.shape[0] * LO // both.shape[1]
+    ids = lax.broadcasted_iota(jnp.int32, (8, first.shape[1]), 0)
     found = lane_lookup(both, jnp.where(ids < 4, first, second))
     target = found[7:8].astype(jnp.int32)
     diff = jnp.where(ids < 3, jnp.concatenate([found[4:8], found[0:4]], axis=0) - found, 0.0)
@@ -110,7 +109,6 @@
     basis = sine * inv
     slope = (order * (math.pi / CUTOFF) * cosine - basis) * inv
     species = jnp.where(ids == jnp.where(ids < 4, kind_src, kind_dst + 4), 1.0, 0.0)
-    feats = 64
     x = jnp.concatenate(
         [
             pick(table_i[...], first, feats).astype(BF16),
@@ -119,29 +117,31 @@
         ],
         axis=0,
     )
-    pre = jnp.dot(wt[...], x, preferred_element_type=F32)
-    hidden, slope_one = silu_parts(pre)
-    pre_two = jnp.dot(wht[...], hidden.astype(BF16), preferred_element_type=F32)
-    top, slope_two = silu_parts(pre_two)
+    hidden, slope_one = silu_parts(jnp.dot(wt[...], x, preferred_element_type=F32))
+    top, slope_two = silu_parts(jnp.dot(wht[...], hidden.astype(BF16), preferred_element_type=F32))
     v = vec[...][:, 0:1]
     score = jnp.sum(top * v, axis=0, keepdims=True)
-    back = jnp.dot(w_hidden[...], (slope_two * v).astype(BF16), preferred_element_type=F32)
-    grad_x = jnp.dot(wb[...], (back * slope_one).astype(BF16), preferred_element_type=F32)
     ratio = jnp.minimum(r * (1.0 / CUTOFF), 1.0)
     rest = 1.0 - ratio * ratio
     envelope = rest * rest * live
-    grad_x = grad_x * envelope
-    grad_r = jnp.sum(grad_x[2 * feats : 2 * feats + 8] * slope, axis=0, keepdims=True)
-    grad_r = grad_r + score * live * (rest * ratio * (-4.0 / CUTOFF))
-    grad_d = diff * (grad_r * inv)
-    grad_d = grad_d + jnp.concatenate([grad_d[4:8], grad_d[0:4]], axis=0)
-    return envelope * score, grad_x[0:feats], grad_x[feats : 2 * feats], grad_d, target
+    by_cutoff = score * live * (rest * ratio * (-4.0 / CUTOFF))
+    way = diff * inv
+    way = way + jnp.concatenate([way[4:8], way[0:4]], axis=0)
+    return envelope * score, slope_one, (slope_two * v).astype(BF16), way, slope, envelope, by_cutoff, target
+
+
+def backward(down, slope_one, way, slope, envelope, by_cutoff, w_hidden, wb, feats):
+    back = jnp.dot(w_hidden, down, preferred_element_type=F32)
+    grad_x = jnp.dot(wb, (back * slope_one).astype(BF16), preferred_element_type=F32) * envelope
+    grad_r = jnp.sum(grad_x[2 * feats : 2 * feats + 8] * slope, axis=0, keepdims=True) + by_cutoff
+    return grad_x[0:feats], grad_x[feats : 2 * feats], way * grad_r
 
 
 def kernel(
     sizes, counts, local_pairs, pairs_x, pairs_y, positions, features, lists, w_rbf, w_src, w_dst, species_src,
     species_dst, w_hidden, w_latent, w_energy, energy_out, sums_out, pairs, tables, lent, lent_n, both, wt, wb,
-    wht, vec, acc_i, acc_j, message, message_n, hold_i, hold_j, hold_d, hold_ids, energy, energy_one, energy_two,
+    wht, vec, acc_i, acc_j, message, message_n, keep_slope, keep_down, keep_rows,
+    keep_ids, hold_i, hold_j, hold_d, energy, energy_one, energy_two,
     got_one, got_two, send_sem, recv_sem, send_one, recv_one, send_two, recv_two,
 ):
     n_gx, n_gy = sizes
@@ -151,7 +151,8 @@
     halo = lists.shape[1]
     n_cross = pairs_x.shape[1] // BLK
     n_all = pairs.shape[1] // BLK
-    start_x, start_y, start_late = EARLY, EARLY + n_cross, EARLY + 2 * n_cross
+    start_x = local_pairs.shape[1] // BLK
+    start_y = start_x + n_cross
 
     def peer(axis, by):
         if axis == 0:
@@ -167,11 +168,9 @@
 
         lax.fori_loop(1, sizes[axis], greet, 0)
 
-    early = EARLY * BLK
-    pairs[:, 0:early] = local_pairs[:, 0:early]
-    pairs[:, early : early + pairs_x.shape[1]] = pairs_x[...]
-    pairs[:, early + pairs_x.shape[1] : start_late * BLK] = pairs_y[...]
-    pairs[:, start_late * BLK :] = local_pairs[:, early:]
+    pairs[:, 0 : start_x * BLK] = local_pairs[...]
+    pairs[:, start_x * BLK : start_y * BLK] = pairs_x[...]
+    pairs[:, start_y * BLK :] = pairs_y[...]
     for h in range(spans):
         tables[0, h * width : (h + 1) * width, :] = features[:, h * LO : (h + 1) * LO]
     place = positions[...]
@@ -187,7 +186,6 @@
     acc_i[...] = jnp.zeros_like(acc_i)
     acc_j[...] = jnp.zeros_like(acc_j)
     energy[...] = jnp.zeros_like(energy)
-    weights = (wt, wb, wht, w_hidden, vec)
 
     def lend(axis, part, source, target, by):
         return pltpu.make_async_remote_copy(
@@ -209,39 +207,14 @@
     returns = [lend(axis, 2, message.at[axis], message_n.at[axis], 1) for axis in (0, 1)]
 
     def side_of(step):
-        cross = jnp.where(step < start_y, 1, 2)
-        return jnp.where(step < start_x, 0, jnp.where(step < start_late, cross, 0))
-
-    def network(step):
-        side = side_of(step)
-        skipped = jnp.where(
-            side == 0, jnp.where(step < start_x, 0, 2 * n_cross), jnp.where(side == 1, start_x, start_y)
-        )
-        block = pairs[:, pl.ds(pl.multiple_of(step * BLK, BLK), BLK)]
-        slot = (step - skipped) * BLK + lax.broadcasted_iota(jnp.int32, (1, BLK), 1)
-        live = jnp.where(slot < counts[0, side], 1.0, 0.0)
-        e, grad_i, grad_j, grad_d, target = pair_block(
-            block[0:1], block[1:2], block[2:3], block[3:4], live, both[side], tables.at[0], tables.at[side], weights
-        )
-        energy[...] += e
-        hold_i[...] = grad_i
-        hold_j[...] = grad_j
-        hold_d[...] = grad_d
-        hold_ids[0:1, :] = block[0:1]
-        hold_ids[1:2, :] = target
-
-    def scatter(step):
-        side = side_of(step)
-        acc_i[...] += scatter_product(hold_i[...], -hold_d[...], hold_ids[0:1, :], spans)
-        acc_j[side] += scatter_product(hold_j[...], hold_d[...], hold_ids[1:2, :], spans)
-
-    network(0)
+        return jnp.where(step < start_x, 0, jnp.where(step < start_y, 1, 2))
+
     pl.semaphore_wait(barrier, n_gx + n_gy - 2)
     for group in halos:
         for copy in group:
             copy.start()
 
-    def visit(step, carry):
+    def ahead(step, carry):
         for axis, begin in ((0, start_x), (1, start_y)):
 
             @pl.when(step == begin)
@@ -253,20 +226,29 @@
                 both[axis + 1] = both[0]
                 both[axis + 1, :, 0:halo] = jnp.where(ids < 4, both[0, :, 0:halo], far)
 
-        scatter(step - 1)
-        network(step)
-        for axis, end in ((0, start_y), (1, start_late)):
-
-            @pl.when(step == end)
-            def _():
-                message[axis] = acc_j[axis + 1].astype(BF16)
-                returns[axis].start()
-
+        side = side_of(step)
+        skipped = jnp.where(side == 0, 0, jnp.where(side == 1, start_x, start_y))
+        block = pairs[:, pl.ds(pl.multiple_of(step * BLK, BLK), BLK)]
+        slot = (step - skipped) * BLK + lax.broadcasted_iota(jnp.int32, (1, BLK), 1)
+        live = jnp.where(slot < counts[0, side], 1.0, 0.0)
+        got = forward(
+            block[0:1], block[1:2], block[2:3], block[3:4], live, both[side], tables.at[0], tables.at[side],
+            (wt, wht, vec),
+        )
+        energy[...] += got[0]
+        keep_slope[step] = got[1]
+        keep_down[step] = got[2]
+        keep_rows[step, 0:8] = got[3]
+        keep_rows[step, 8:16] = got[4]
+        keep_rows[step, 16:17] = got[5]
+        keep_rows[step, 17:18] = got[6]
+        keep_ids[step, 0:1] = block[0:1]
+        keep_ids[step, 1:2] = got[7]
         return carry
 
-    lax.fori_loop(1, n_all, visit, 0)
-
-    def exchange(axis, value, source, target, send, recv):
+    lax.fori_loop(0, n_all, ahead, 0)
+
+    def exchange(axis, source, target, send, recv):
         def copy_of(by):
             return pltpu.make_async_remote_copy(
                 src_ref=source,
@@ -285,16 +267,55 @@
             copy_of(by).wait()
             return carry
 
-        source[...] = value
-        lax.fori_loop(1, sizes[axis], start, 0)
-        return lambda: lax.fori_loop(1, sizes[axis], wait, 0)
-
-    total = jnp.broadcast_to(jnp.sum(energy[...], axis=1, keepdims=True), energy_one.shape)
-    wait_one = exchange(1, total, energy_one, got_one, send_one, recv_one)
+        return (
+            lambda: lax.fori_loop(1, sizes[axis], start, 0),
+            lambda: lax.fori_loop(1, sizes[axis], wait, 0),
+        )
+
+    start_one, wait_one = exchange(1, energy_one, got_one, send_one, recv_one)
+    start_two, wait_two = exchange(0, energy_two, got_two, send_two, recv_two)
+    energy_one[...] = jnp.broadcast_to(jnp.sum(energy[...], axis=1, keepdims=True), energy_one.shape)
+    start_one()
+
+    def place_of(turn):
+        return jnp.where(turn < 2 * n_cross, start_x + turn, turn - 2 * n_cross)
+
+    def network(turn):
+        step = place_of(turn)
+        rows = keep_rows[step]
+        hold_i[...], hold_j[...], hold_d[...] = backward(
+            keep_down[step], keep_slope[step], rows[0:8], rows[8:16], rows[16:17], rows[17:18], w_hidden[...], wb[...],
+            width,
+        )
+
+    def scatter(turn):
+        step = place_of(turn)
+        ids = keep_ids[step]
+        acc_i[...] += scatter_product(hold_i[...], -hold_d[...], ids[0:1], spans)
+        acc_j[side_of(step)] += scatter_product(hold_j[...], hold_d[...], ids[1:2], spans)
+
+    network(0)
+
+    def behind(turn, carry):
+        scatter(turn - 1)
+        network(turn)
+        for axis in (0, 1):
+
+            @pl.when(turn == (axis + 1) * n_cross)
+            def _():
+                message[axis] = acc_j[axis + 1].astype(BF16)
+                returns[axis].start()
+
+        @pl.when(turn == n_all // 2)
+        def _():
+            wait_one()
+            energy_two[...] = energy_one[...] + jnp.sum(got_one[1:n_gy], axis=0)
+            start_two()
+
+        return carry
+
+    lax.fori_loop(1, n_all, behind, 0)
     scatter(n_all - 1)
-    wait_one()
-    total = total + jnp.sum(got_one[1:n_gy], axis=0)
-    wait_two = exchange(0, total, energy_two, got_two, send_two, recv_two)
     for group in halos:
         for copy in group:
             copy.wait_send()
@@ -302,7 +323,7 @@
         back.wait()
     sums_out[...] = acc_i[...] + acc_j[0] + message_n[0].astype(F32) + message_n[1].astype(F32)
     wait_two()
-    total = total + jnp.sum(got_two[1:n_gx], axis=0)
+    total = energy_two[...] + jnp.sum(got_two[1:n_gx], axis=0)
     energy_out[...] = total[0:1, 0:1] / (atoms * n_gx * n_gy)
 
 
@@ -352,15 +373,18 @@
             pltpu.VMEM((3, rows, LO), F32),
             pltpu.VMEM((2, rows, LO), BF16),
             pltpu.VMEM((2, rows, LO), BF16),
+            pltpu.VMEM((slots // BLK, hid, BLK), F32),
+            pltpu.VMEM((slots // BLK, hid, BLK), BF16),
+            pltpu.VMEM((slots // BLK, 24, BLK), F32),
+            pltpu.VMEM((slots // BLK, 8, BLK), jnp.int32),
             pltpu.VMEM((width, BLK), F32),
             pltpu.VMEM((width, BLK), F32),
             pltpu.VMEM((8, BLK), F32),
-            pltpu.VMEM((8, BLK), jnp.int32),
             pltpu.VMEM((1, BLK), F32),
-            pltpu.VMEM((8, 128), F32),
-            pltpu.VMEM((8, 128), F32),
-            pltpu.VMEM((n_gy, 8, 128), F32),
-            pltpu.VMEM((n_gx, 8, 128), F32),
+            pltpu.VMEM((1, 128), F32),
+            pltpu.VMEM((1, 128), F32),
+            pltpu.VMEM((n_gy, 1, 128), F32),
+            pltpu.VMEM((n_gx, 1, 128), F32),
             dma((2, 3)),
             dma((2, 3)),
             dma((n_gy,)),

time: 54 us -> 46.1 us (0.85)
  Pallas kernels: 53.2 us -> 45.3 us
    pallas_call x1, Pallas kernels: 50.7 us -> 42.8 us  [on_device(): pl.pallas_call(functools.partial(kernel, (n_gx, n_gy)), in_specs=[pl.Bloc...]
where the time goes in v5:
time: 46.1 us; the launch traced here: 45.9 us
  Pallas kernels  45.3 us (98%)
  between operations  0.65 us (1%)
    pallas_call x1, Pallas kernels, on_device(): pl.pallas_call(functools.partial(kernel, (n_gx, n_gy)), in_specs=[pl.Bloc...  42.8 us
    pallas_call x1, Pallas kernels, on_device(): pl.pallas_call(finish, in_specs=[vmem] * 2, out_specs=[vmem] * 3, out_sha...  2.45 us

profile of v5, /device:TPU:1, one launch (start us, length us, event | category | flops | bytes accessed | tf_op | source)
XLA Modules:
  0.0 45.9 jit_solution(16524047088428199697)
XLA Ops:
  0.6 42.8 %shard_map.166 = (f32[1,1]{1,0:T(1,128)}, f32[544,256]{1,0:T(8,128)}) custom-call(s32[1,3]{1,0:T(1,128)} %counts.1, s32[4,6144]{1,0:T(4,128)} %local_pairs.1, s32[4,2048]{1,0:T(4,128)} %pairs_x.1, s32[4,2048]{1,0:T(4,128)} %pairs_y.1, f32[3,2048]{1,0:T(4,128)} %positions.1, bf16[64,2048]{1,0:T(8,128)(2,1)} %features.1, s32[2,1536]{1,0:T(2,128)} %lists.1, ...), custom_call_target="tpu_custom_call" | custom-call | flops 30000001024 | bytes 4000000 | tf_op jit(solution)/shard_map/pallas_call | solution.py:357
  43.5 2.4 %shard_map.167 = (f32[1,1]{1,0:T(1,128)}, f32[3,2048]{1,0:T(4,128)}, f32[64,2048]{1,0:T(8,128)}) custom-call(f32[1,1]{1,0:T(1,128)} %get-tuple-element.8.energy_in, f32[544,256]{1,0:T(8,128)} %get-tuple-element.9.sums), custom_call_target="tpu_custom_call" | custom-call | flops 1000000 | bytes 2000000 | tf_op jit(solution)/shard_map/pallas_call | solution.py:403

commit v6 on v5

--- a/solution.py
+++ b/solution.py
@@ -19,10 +19,10 @@
 MESH = pl.DeviceIdType.MESH
 
 
-def silu_parts(x):
-    sig = 0.5 * jnp.tanh(0.5 * x) + 0.5
-    y = x * sig
-    return y, sig + y * (1.0 - sig)
+def silu_parts(z):
+    u = jnp.tanh(z) + 1.0
+    y = z * u
+    return y, u + y * (2.0 - u)
 
 
 def sin_cos_pi(y):
@@ -88,9 +88,9 @@
     stack = jnp.concatenate(
         [a[...].astype(F32) for a in (w_src, w_dst, w_rbf, species_src, species_dst)], axis=0
     )
-    wb[...] = stack.astype(BF16)
-    wt[...] = stack.T.astype(BF16)
-    wht[...] = w_hidden[...].astype(F32).T.astype(BF16)
+    wb[...] = (stack * 0.25).astype(BF16)
+    wt[...] = (stack * 0.5).T.astype(BF16)
+    wht[...] = (w_hidden[...].astype(F32) * 0.5).T.astype(BF16)
     score = jnp.sum(w_latent_t[...].astype(F32).T * w_energy[...], axis=1, keepdims=True)
     vec[...] = jnp.broadcast_to(score, vec.shape)
 
@@ -118,16 +118,19 @@
         axis=0,
     )
     hidden, slope_one = silu_parts(jnp.dot(wt[...], x, preferred_element_type=F32))
-    top, slope_two = silu_parts(jnp.dot(wht[...], hidden.astype(BF16), preferred_element_type=F32))
-    v = vec[...][:, 0:1]
-    score = jnp.sum(top * v, axis=0, keepdims=True)
+    half = jnp.dot(wht[...], hidden.astype(BF16), preferred_element_type=F32)
+    u = jnp.tanh(half) + 1.0
+    scaled = u * vec[...][:, 0:1]
+    top = half * scaled
+    score = jnp.sum(top, axis=0, keepdims=True)
+    down = (scaled + top * (2.0 - u)).astype(BF16)
     ratio = jnp.minimum(r * (1.0 / CUTOFF), 1.0)
     rest = 1.0 - ratio * ratio
     envelope = rest * rest * live
     by_cutoff = score * live * (rest * ratio * (-4.0 / CUTOFF))
     way = diff * inv
     way = way + jnp.concatenate([way[4:8], way[0:4]], axis=0)
-    return envelope * score, slope_one, (slope_two * v).astype(BF16), way, slope, envelope, by_cutoff, target
+    return envelope * score, slope_one, down, way, slope, envelope, by_cutoff, target
 
 
 def backward(down, slope_one, way, slope, envelope, by_cutoff, w_hidden, wb, feats):

time: 46.1 us -> 44.7 us (0.970)
  Pallas kernels: 45.3 us -> 43.9 us
    pallas_call x1, Pallas kernels: 42.8 us -> 41.5 us  [on_device(): pl.pallas_call(functools.partial(kernel, (n_gx, n_gy)), in_specs=[pl.Bloc...]
where the time goes in v6:
time: 44.7 us; the launch traced here: 44.6 us
  Pallas kernels  43.9 us (98%)
  between operations  0.65 us (1%)
    pallas_call x1, Pallas kernels, on_device(): pl.pallas_call(functools.partial(kernel, (n_gx, n_gy)), in_specs=[pl.Bloc...  41.5 us
    pallas_call x1, Pallas kernels, on_device(): pl.pallas_call(finish, in_specs=[vmem] * 2, out_specs=[vmem] * 3, out_sha...  2.45 us

profile of v6, /device:TPU:1, one launch (start us, length us, event | category | flops | bytes accessed | tf_op | source)
XLA Modules:
  0.0 44.6 jit_solution(12599185889560651159)
XLA Ops:
  0.6 41.5 %shard_map.166 = (f32[1,1]{1,0:T(1,128)}, f32[544,256]{1,0:T(8,128)}) custom-call(s32[1,3]{1,0:T(1,128)} %counts.1, s32[4,6144]{1,0:T(4,128)} %local_pairs.1, s32[4,2048]{1,0:T(4,128)} %pairs_x.1, s32[4,2048]{1,0:T(4,128)} %pairs_y.1, f32[3,2048]{1,0:T(4,128)} %positions.1, bf16[64,2048]{1,0:T(8,128)(2,1)} %features.1, s32[2,1536]{1,0:T(2,128)} %lists.1, ...), custom_call_target="tpu_custom_call" | custom-call | flops 30000001024 | bytes 4000000 | tf_op jit(solution)/shard_map/pallas_call | solution.py:360
  42.1 2.4 %shard_map.167 = (f32[1,1]{1,0:T(1,128)}, f32[3,2048]{1,0:T(4,128)}, f32[64,2048]{1,0:T(8,128)}) custom-call(f32[1,1]{1,0:T(1,128)} %get-tuple-element.8.energy_in, f32[544,256]{1,0:T(8,128)} %get-tuple-element.9.sums), custom_call_target="tpu_custom_call" | custom-call | flops 1000000 | bytes 2000000 | tf_op jit(solution)/shard_map/pallas_call | solution.py:406

commit v7 on v6

--- a/solution.py
+++ b/solution.py
@@ -57,9 +57,9 @@
 
 
 def one_hot(index):
-    low = (index & (LO - 1)).astype(F32)
-    rows = lax.broadcasted_iota(jnp.int32, (LO, index.shape[1]), 0).astype(F32)
-    return jnp.where(rows == low, 1.0, 0.0).astype(BF16)
+    low = (index & (LO - 1)).astype(F32).astype(BF16)
+    rows = lax.broadcasted_iota(jnp.int32, (LO, index.shape[1]), 0).astype(F32).astype(BF16)
+    return jnp.where(rows == low, jnp.ones((), BF16), jnp.zeros((), BF16))
 
 
 def pick(table, index, width):
@@ -74,7 +74,9 @@
 def scatter_product(feat, place, index, spans):
     hi = index >> 8
     half = lax.broadcasted_iota(jnp.int32, place.shape, 0) >> 2
-    parts = [jnp.where(hi == h, feat, 0.0).astype(BF16) for h in range(spans)]
+    near = hi.astype(F32).astype(BF16)
+    small = feat.astype(BF16)
+    parts = [jnp.where(near == h, small, jnp.zeros((), BF16)) for h in range(spans)]
     pairs = [jnp.where(hi == 2 * g + half, place, 0.0) for g in range(spans // 2)]
     parts.append(jnp.concatenate(pairs, axis=0).astype(BF16))
     wide = jnp.concatenate(parts, axis=0)

time: 44.7 us -> 44.6 us (level)
  no operation moved by 1% of the time
where the time goes in v7:
time: 44.6 us; the launch traced here: 44.5 us
  Pallas kernels  43.8 us (98%)
  between operations  0.65 us (1%)
    pallas_call x1, Pallas kernels, on_device(): pl.pallas_call(functools.partial(kernel, (n_gx, n_gy)), in_specs=[pl.Bloc...  41.4 us
    pallas_call x1, Pallas kernels, on_device(): pl.pallas_call(finish, in_specs=[vmem] * 2, out_specs=[vmem] * 3, out_sha...  2.45 us

profile of v7, /device:TPU:1, one launch (start us, length us, event | category | flops | bytes accessed | tf_op | source)
XLA Modules:
  0.0 44.5 jit_solution(6538630421628234615)
XLA Ops:
  0.6 41.4 %shard_map.166 = (f32[1,1]{1,0:T(1,128)}, f32[544,256]{1,0:T(8,128)}) custom-call(s32[1,3]{1,0:T(1,128)} %counts.1, s32[4,6144]{1,0:T(4,128)} %local_pairs.1, s32[4,2048]{1,0:T(4,128)} %pairs_x.1, s32[4,2048]{1,0:T(4,128)} %pairs_y.1, f32[3,2048]{1,0:T(4,128)} %positions.1, bf16[64,2048]{1,0:T(8,128)(2,1)} %features.1, s32[2,1536]{1,0:T(2,128)} %lists.1, ...), custom_call_target="tpu_custom_call" | custom-call | flops 30000001024 | bytes 4000000 | tf_op jit(solution)/shard_map/pallas_call | solution.py:362
  42.0 2.4 %shard_map.167 = (f32[1,1]{1,0:T(1,128)}, f32[3,2048]{1,0:T(4,128)}, f32[64,2048]{1,0:T(8,128)}) custom-call(f32[1,1]{1,0:T(1,128)} %get-tuple-element.8.energy_in, f32[544,256]{1,0:T(8,128)} %get-tuple-element.9.sums), custom_call_target="tpu_custom_call" | custom-call | flops 1000000 | bytes 2000000 | tf_op jit(solution)/shard_map/pallas_call | solution.py:408
